TPU v7x, 32 devices: a whole 2x2x4 slice. The times are simulated.
32 devices in a mesh: scene: 2 (over core), seq: 16 (over z, y, x).
Axes of the slice: x: 2, y: 2, z: 4, core: 2. Of those that a mesh axis runs over, the one named last changes fastest.
Arguments:
- points: bfloat16 [131072, 512], P(('scene', 'seq')), parts along dimension 0, may hold values from -6 to 6
- order: int32 [1024], P(('scene', 'seq')), parts along dimension 0, may hold values from 0 to 511, as said below
- offsets: int32 [128], P(('scene', 'seq')), parts along dimension 0, may hold values from -2 to 2, as said below
- norm_gain: float32 [512], replicated, may hold values from 0.25 to 1.75
- w_qkv: bfloat16 [512, 1536], replicated, may hold values from -8 to 8
- w_out: bfloat16 [512, 512], replicated, may hold values from -0.25 to 0.25
Outputs:
- mixed: bfloat16 [131072, 512], P(('scene', 'seq')), parts along dimension 0
There are 2 independent parts, one for each index of `scene`. A program takes and returns all parts, laid end to end along the dimension named above; an argument that names none is the same for every part. Nothing has to cross between parts.
Inputs may be any that keep to these rules, and one draw needn't show every extreme that they name: `order`: a permutation of 0 to 511; among the blocks of one device at most 2 take serial positions in one range e * 32 to (e + 1) * 32 - 1, and some device has exactly 2 in one such range. `offsets`: never zero; both minus 2 and 2 occur.
All inputs are finite; a program needn't handle non-finite values.
Results may differ from a plain program's by a relative error of at most 0.0049.
Values may be sent and summed in bfloat16 or wider, within the bound.
No kernel may reach another device: no remote copies, remote signals or barrier semaphores. Data moves between devices by JAX's collectives and lax.ppermute only.
A program may use at most 192 MiB of HBM per device.

v0:
```python
import math

import jax
import jax.numpy as jnp
from jax import lax
from jax.sharding import PartitionSpec as P

HEADS = 8


def passed_along(value, axis, steps):
    count = lax.axis_size(axis)
    pairs = [(source, (source + steps) % count) for source in range(count)]
    return lax.ppermute(value, axis, pairs)


def layer_norm(row_block, norm_gain):
    values = row_block.astype(jnp.float32)
    centre = jnp.mean(values, axis=-1, keepdims=True)
    spread = jnp.mean(jnp.square(values - centre), axis=-1, keepdims=True)
    return ((values - centre) * lax.rsqrt(spread + 1e-05) * norm_gain).astype(jnp.bfloat16)


def attend_one(operands):
    queries, key_block, value_block = operands
    scores = jnp.dot(queries, key_block.T, preferred_element_type=jnp.float32) / math.sqrt(
        queries.shape[-1]
    )
    row_max = jnp.max(scores, axis=-1, keepdims=True)
    raised = jnp.exp(scores - row_max)
    weights = (raised / jnp.sum(raised, axis=-1, keepdims=True)).astype(jnp.bfloat16)
    return jnp.dot(weights, value_block, preferred_element_type=jnp.float32).astype(jnp.bfloat16)


def heads_first(row_block, head_count):
    total, length, features = row_block.shape
    split = row_block.reshape(total, length, head_count, features // head_count)
    return split.transpose(0, 2, 1, 3).reshape(total * head_count, length, features // head_count)


def patch_attention(queries, key_sets, value_sets, head_count):
    total, length, features = queries.shape
    result = lax.map(
        attend_one,
        (
            heads_first(queries, head_count),
            heads_first(key_sets, head_count),
            heads_first(value_sets, head_count),
        ),
    )
    result = result.reshape(total, head_count, length, features // head_count)
    return result.transpose(0, 2, 1, 3).reshape(total * length, features)


def body(points, order, offsets, norm_gain, w_qkv, w_out):
    features = points.shape[1]
    block_count = order.shape[0]
    block_rows = points.shape[0] // block_count
    shards = lax.axis_size("seq")
    capacity = (block_count + shards - 1) // shards
    blocks = points.reshape(block_count, block_rows, features)
    target = order // block_count
    local_pos = order % block_count
    block_ids = jnp.arange(block_count, dtype=jnp.int32)
    earlier = (target[None, :] == target[:, None]) & (block_ids[None, :] < block_ids[:, None])
    slot_pos = target * capacity + jnp.sum(earlier.astype(jnp.int32), axis=1)
    slot_ids = jnp.arange(shards * capacity, dtype=jnp.int32)
    matches = slot_ids[:, None] == slot_pos[None, :]
    filled = jnp.any(matches, axis=1)
    source_ids = jnp.sum(jnp.where(matches, block_ids[None, :], 0), axis=1)
    outgoing = jnp.where(filled[:, None, None], blocks[source_ids], jnp.zeros((), jnp.bfloat16))
    outgoing_pos = jnp.where(filled, local_pos[source_ids], -1)
    arrived, arrived_pos = (
        lax.all_to_all(outgoing, "seq", split_axis=0, concat_axis=0, tiled=True),
        lax.all_to_all(outgoing_pos, "seq", split_axis=0, concat_axis=0, tiled=True),
    )
    arrival_ids = jnp.arange(arrived_pos.shape[0], dtype=jnp.int32)
    picked = jnp.sum(
        jnp.where(arrived_pos[None, :] == block_ids[:, None], arrival_ids[None, :], 0), axis=1
    )
    serial = arrived[picked].reshape(-1, features)
    row_total = serial.shape[0]
    patch_count = offsets.shape[0]
    patch_rows = row_total // patch_count
    normed = layer_norm(serial, norm_gain)
    projected = jnp.dot(normed, w_qkv, preferred_element_type=jnp.float32).astype(jnp.bfloat16)
    own_pair = jnp.stack([projected[:, features : 2 * features], projected[:, 2 * features :]])
    from_left = passed_along(own_pair, "seq", 1)
    from_right = passed_along(own_pair, "seq", -1)
    stacked = jnp.concatenate([from_left, own_pair, from_right], axis=1)
    stacked = stacked.reshape(2, -1, patch_rows, features)
    partner_index = patch_count + jnp.arange(patch_count, dtype=jnp.int32) + offsets
    partner = stacked[:, partner_index]
    own_patches = own_pair.reshape(2, patch_count, patch_rows, features)
    key_value_sets = jnp.concatenate([own_patches, partner], axis=2)
    queries = projected[:, :features].reshape(patch_count, patch_rows, features)
    attended = patch_attention(queries, key_value_sets[0], key_value_sets[1], HEADS)
    serial_out = (
        serial.astype(jnp.float32) + jnp.dot(attended, w_out, preferred_element_type=jnp.float32)
    ).astype(jnp.bfloat16)
    out_blocks = serial_out.reshape(block_count, block_rows, features)
    returning = jnp.where(
        (arrived_pos >= 0)[:, None, None],
        out_blocks[jnp.maximum(arrived_pos, 0)],
        jnp.zeros((), jnp.bfloat16),
    )
    homeward = lax.all_to_all(returning, "seq", split_axis=0, concat_axis=0, tiled=True)
    return homeward[slot_pos].reshape(-1, features)


def solution(mesh):
    return jax.shard_map(
        body,
        mesh=mesh,
        in_specs=(
            P(("scene", "seq"), None),
            P(("scene", "seq")),
            P(("scene", "seq")),
            P(),
            P(),
            P(),
        ),
        out_specs=P(("scene", "seq"), None),
        check_vma=False,
    )
```

profile of v0, /device:TPU:12, one launch (start us, length us, event | category | flops | bytes accessed | tf_op | source)
XLA Modules:
  0.0 989.5 jit_solution(2759074679828428130)
XLA Ops:
  3.2 7.2 all-to-all-start
  10.4 5.0 gather_fusion.1
  15.4 4.5 broadcast_select_fusion
  20.0 6.9 all-to-all-start.1
  28.3 91.3 %all-to-all-done.1 = bf16[32,128,512]{2,1,0:T(8,128)(2,1)} async-done(((bf16[32,128,512]{2,1,0:T(8,128)(2,1)}), bf16[32,128,512]{2,1,0:T(8,128)(2,1)}, u32[]{:S(2)}, u32[]{:S(2)}) %all-to-all-start.1) | async-done | bytes 4194336 | tf_op jit(solution)/shard_map/all_to_all | solution.py:74
  119.6 5.0 gather_fusion.2
  131.3 7.0 convolution_convert_fusion
  138.3 6.1 fusion.28
  144.4 7.7 pad_maximum_fusion.2
  156.3 6.3 copy.42
  162.6 6.3 copy.43
  168.9 6.4 copy.40
  175.3 7.8 reshape_reshape.3
  183.1 10.7 %copy.50 = bf16[4,8,1024,64]{3,2,1,0:T(8,128)(2,1)} copy(bf16[4,8,1024,64]{2,0,3,1:T(4,128)(2,1)} %bitcast.91) | data formatting | bytes 8388608 | tf_op jit(solution)/shard_map/reshape | solution.py:38
  193.7 143.0 %collective-permute-done = bf16[2,4096,512]{2,1,0:T(8,128)(2,1)} collective-permute-done((bf16[2,4096,512]{2,1,0:T(8,128)(2,1)}, bf16[2,4096,512]{2,1,0:T(8,128)(2,1)}, u32[]{:S(2)}, u32[]{:S(2)}) %collective-permute-start) | collective-permute-done | bytes 8388640 | tf_op jit(solution)/shard_map/ppermute | solution.py:14
  336.7 176.2 %collective-permute-done.1 = bf16[2,4096,512]{2,1,0:T(8,128)(2,1)} collective-permute-done((bf16[2,4096,512]{2,1,0:T(8,128)(2,1)}, bf16[2,4096,512]{2,1,0:T(8,128)(2,1)}, u32[]{:S(2)}, u32[]{:S(2)}) %collective-permute-start.1) | collective-permute-done | bytes 8388640 | tf_op jit(solution)/shard_map/ppermute | solution.py:14
  512.9 24.1 %pad_maximum_fusion = bf16[2,12288,512]{2,1,0:T(8,128)(2,1)} fusion(bf16[2,4096,512]{2,1,0:T(8,128)(2,1)} %collective-permute-done.1, bf16[1,4096,512]{2,1,0:T(8,128)(2,1)} %get-tuple-element.75, bf16[1,4096,512]{2,1,0:T(8,128)(2,1)} %copy-done.4, bf16[2,4096,512]{2,1,0:T(8,128)(2,1)} %collective-permute-done), kind=kLoop, calls=%fused_computation.25 | loop fusion | flops 100663296 | bytes 50331648 | tf_op jit(solution)/shard_map/concatenate | solution.py:90
  537.0 17.0 %fusion.26 = (bf16[2,12,512,512]{3,2,1,0:T(8,128)(2,1)}, bf16[2,12,512,512]{3,2,1,0:T(8,128)(2,1)}) fusion(bf16[2,12,1024,512]{3,2,1,0:T(8,128)(2,1)} %bitcast.90), kind=kLoop, calls=%fused_computation.74 | loop fusion | bytes 50331648 | tf_op jit(solution)/shard_map/gather | solution.py:93
  554.0 7.3 gather_fusion.5
  561.3 7.3 copy.44
  568.6 7.3 gather_fusion.6
  575.9 7.2 copy.45
  583.2 8.1 pad_maximum_fusion.1
  591.2 6.3 fusion.27
  597.6 266.8 %while.10 = (s32[]{:T(128)}, bf16[32,1024,64]{1,2,0:T(8,128)(2,1)}, bf16[32,1024,64]{2,1,0:T(8,128)(2,1)}, bf16[32,2048,64]{1,2,0:T(8,128)(2,1)}, bf16[32,2048,64]{1,2,0:T(8,128)(2,1)}, /*index=5*/s32[]{:T(128)}) while((s32[]{:T(128)}, bf16[32,1024,64]{1,2,0:T(8,128)(2,1)}, bf16[32,1024,64]{2,1,0:T(8,128)(2,1)}, ...), condition=%wide.region_9.10_spmd, body=%wide.region_6.9_spmd.sunk | while | flops 555808768 | bytes 26105924 | solution.py:43
  601.8 4.1 fusion.38
  610.2 4.1 fusion.38
  618.5 4.1 fusion.38
  626.9 4.1 fusion.38
  635.2 4.0 fusion.38
  643.5 4.1 fusion.38
  651.9 4.1 fusion.38
  660.2 4.1 fusion.38
  668.5 4.1 fusion.38
  676.9 4.1 fusion.38
  685.2 4.1 fusion.38
  693.6 4.1 fusion.38
  701.9 4.1 fusion.38
  710.3 4.1 fusion.38
  718.6 4.1 fusion.38
  726.9 4.1 fusion.38
  735.3 4.1 fusion.38
  743.6 4.1 fusion.38
  751.9 4.1 fusion.38
  760.3 4.1 fusion.38
  768.6 4.1 fusion.38
  777.0 4.0 fusion.38
  785.3 4.1 fusion.38
  793.6 4.1 fusion.38
  802.0 4.1 fusion.38
  810.3 4.1 fusion.38
  818.6 4.1 fusion.38
  827.0 4.0 fusion.38
  835.3 4.1 fusion.38
  843.6 4.1 fusion.38
  852.0 4.1 fusion.38
  860.3 4.1 fusion.38
  864.4 5.4 copy.49
  872.3 4.6 fusion.20
  876.9 5.0 gather_fusion.3
  881.9 4.5 broadcast_select_fusion.1
  886.5 6.3 all-to-all-start.2
  892.8 91.7 %all-to-all-done.2 = bf16[32,128,512]{2,1,0:T(8,128)(2,1)} async-done(((bf16[32,128,512]{2,1,0:T(8,128)(2,1)}), bf16[32,128,512]{2,1,0:T(8,128)(2,1)}, u32[]{:S(2)}, u32[]{:S(2)}) %all-to-all-start.2) | async-done | bytes 4194336 | tf_op jit(solution)/shard_map/all_to_all | solution.py:107
  984.4 5.0 gather_fusion.4
  (116 shorter events, 154.6 us)
Async XLA Ops:
  0.0 131.3 %copy-start = (bf16[512,1536]{1,0:T(8,128)(2,1)S(1)}, bf16[512,1536]{1,0:T(8,128)(2,1)}, u32[]{:S(2)}) copy-start(bf16[512,1536]{1,0:T(8,128)(2,1)} %param.12) | copy-start | bytes 4718596
  3.2 16.7 %all-to-all-start = ((s32[16,2,1]{1,2,0:T(1,128)}), s32[16,2,1]{1,2,0:T(1,128)S(1)}, u32[]{:S(2)}, u32[]{:S(2)}) async-start(s32[16,2,1]{1,2,0:T(1,128)} %bitcast.6), calls=%async_computation | async-start | bytes 16384 | tf_op jit(solution)/shard_map/all_to_all | solution.py:75
  20.0 99.7 %all-to-all-start.1 = ((bf16[32,128,512]{2,1,0:T(8,128)(2,1)}), bf16[32,128,512]{2,1,0:T(8,128)(2,1)}, u32[]{:S(2)}, u32[]{:S(2)}) async-start(bf16[32,128,512]{2,1,0:T(8,128)(2,1)} %broadcast_select_fusion), calls=%async_computation.1 | async-start | bytes 8388608 | tf_op jit(solution)/shard_map/all_to_all | solution.py:74
  124.7 3.4 copy-start.2
  124.7 5.2 copy-start.5
  144.4 7.7 copy-start.4
  144.4 10.6 %copy-start.9 = (s32[4]{0:T(128)S(1)}, s32[4]{0:T(128)}, u32[]{:S(2)}) copy-start(s32[4]{0:T(128)} %param.10) | copy-start | bytes 52
  152.1 184.6 %collective-permute-start = (bf16[2,4096,512]{2,1,0:T(8,128)(2,1)}, bf16[2,4096,512]{2,1,0:T(8,128)(2,1)}, u32[]{:S(2)}, u32[]{:S(2)}) collective-permute-start(bf16[2,4096,512]{2,1,0:T(8,128)(2,1)} %pad_maximum_fusion.2), channel_id=1, source_target_pairs={{0,1},{1,2},{2,3},{3,4},{4,5},{5,6},{6,7},{7,8},{8,9},{9,10},{10,1... | collective-permute-start | bytes 25165832 | tf_op jit(solution)/shard_map/ppermute | solution.py:14
  153.9 359.0 %collective-permute-start.1 = (bf16[2,4096,512]{2,1,0:T(8,128)(2,1)}, bf16[2,4096,512]{2,1,0:T(8,128)(2,1)}, u32[]{:S(2)}, u32[]{:S(2)}) collective-permute-start(bf16[2,4096,512]{2,1,0:T(8,128)(2,1)} %pad_maximum_fusion.2), channel_id=1, source_target_pairs={{0,15},{1,0},{2,1},{3,2},{4,3},{5,4},{6,5},{7,6},{8,7},{9,8},{10,9... | collective-permute-start | bytes 25165832 | tf_op jit(solution)/shard_map/ppermute | solution.py:14
  869.8 2.4 copy-start.3
  869.8 2.4 copy-start.8
  876.9 5.1 copy-start.7
  886.5 6.3 copy-start.6
  886.5 98.0 %all-to-all-start.2 = ((bf16[32,128,512]{2,1,0:T(8,128)(2,1)}), bf16[32,128,512]{2,1,0:T(8,128)(2,1)}, u32[]{:S(2)}, u32[]{:S(2)}) async-start(bf16[32,128,512]{2,1,0:T(8,128)(2,1)} %broadcast_select_fusion.1), calls=%async_computation.2 | async-start | bytes 8388608 | tf_op jit(solution)/shard_map/all_to_all | solution.py:107
  892.7 96.7 %copy-start.1 = (bf16[512,1536]{1,0:T(8,128)(2,1)S(1)}, bf16[512,1536]{1,0:T(8,128)(2,1)}, u32[]{:S(2)}) copy-start(bf16[512,1536]{1,0:T(8,128)(2,1)} %param.12) | copy-start | bytes 4718596
where the time goes:
time: 993 us; the launch traced here: 989 us
  waiting for transfers between devices  502 us (51%)
  matrix products  216 us (22%)
  local copies, waits for them, and re-layouts  126 us (13%)
  other arithmetic  121 us (12%)
  starting transfers between devices  23.3 us (2%)
    ppermute x2, waiting for transfers between devices, passed_along(): return lax.ppermute(value, axis, pairs)  319 us
    dot_general x32, matrix products, attend_one(): jnp.dot(weights, value_block, preferred_element_type=jnp.float32)  130 us
    all_to_all x1, waiting for transfers between devices, body(): lax.all_to_all(returning, 'seq', split_axis=0, concat_axis=0, tiled=True)  91.7 us
    all_to_all x1, waiting for transfers between devices, body(): lax.all_to_all(outgoing, 'seq', split_axis=0, concat_axis=0, tiled=True)  91.3 us
    dot_general x32, matrix products, attend_one(): jnp.dot(queries, key_block.T, preferred_element_type=jnp.float32)  74.8 us
    reduce_sum x32, other arithmetic, attend_one(): jnp.sum(raised, axis=-1, keepdims=True)  61.9 us
    gather x5, local copies, waits for them, and re-layouts, body(): partner = stacked[:, partner_index]  46.1 us
    concatenate x1, other arithmetic, body(): stacked = jnp.concatenate([from_left, own_pair, from_right], axis=1)  24.1 us
  transfers between devices with their start and end apart: 5, of which 4 were waited for; matrix products, arithmetic and copies ran while one was open for 5% of the time, Pallas kernels for 0%

commit v1 on v0

v1 whole, which is shorter than its diff:
```python
import functools
import math

import jax
import jax.numpy as jnp
from jax import lax
from jax.experimental import pallas as pl
from jax.experimental.pallas import tpu as pltpu
from jax.sharding import PartitionSpec as P

HEADS = 8
REACH = 2
KEY_TILE = 512
QUERY_TILE = 256
ONES_ROWS = 16
SAFE_SCORE = 80.0
VMEM_BYTES = 56 * 1024 * 1024
BF = jnp.bfloat16
F32 = jnp.float32


def ring_order(count):
    grids = {16: (4, 2, 2), 64: (4, 4, 4)}
    if count not in grids:
        return list(range(count))
    deep, tall, wide = grids[count]
    columns = [(0, x) for x in range(wide)]
    for y in range(1, tall):
        across = range(wide - 1, 0, -1) if y % 2 else range(1, wide)
        columns += [(y, x) for x in across]
    columns += [(y, 0) for y in range(tall - 1, 0, -1)]
    ring = []
    for at, (y, x) in enumerate(columns):
        along = range(deep) if at % 2 == 0 else range(deep - 1, -1, -1)
        ring += [(z * tall + y) * wide + x for z in along]
    return ring


def params(**more):
    return pltpu.CompilerParams(vmem_limit_bytes=VMEM_BYTES, **more)


def moved_blocks(source, index, name):
    count = index.shape[0]

    def kernel(index_ref, source_ref, out_ref, sems):
        copies = [
            pltpu.make_async_copy(source_ref.at[index_ref[i]], out_ref.at[i], sems.at[i]) for i in range(count)
        ]
        for copy in copies:
            copy.start()
        for copy in copies:
            copy.wait()

    return pl.pallas_call(
        kernel,
        grid_spec=pltpu.PrefetchScalarGridSpec(
            num_scalar_prefetch=1,
            grid=(1,),
            in_specs=[pl.BlockSpec(memory_space=pl.ANY)],
            out_specs=pl.BlockSpec(memory_space=pl.ANY),
            scratch_shapes=[pltpu.SemaphoreType.DMA((count,))],
        ),
        out_shape=jax.ShapeDtypeStruct((count,) + source.shape[1:], source.dtype),
        name=name,
    )(index, source)


def norm_kernel(picked_ref, *refs):
    *block_refs, gain_ref, low_ref, high_ref = refs
    patch = pl.program_id(0)
    half = pl.num_programs(0) // 2

    def write(out_ref):
        for i, block_ref in enumerate(block_refs):
            length = block_ref.shape[1]
            values = block_ref[0].astype(F32)
            centred = values - jnp.mean(values, axis=-1, keepdims=True)
            spread = jnp.mean(jnp.square(centred), axis=-1, keepdims=True)
            out_ref[i * length : (i + 1) * length, :] = (
                centred * lax.rsqrt(spread + 1e-05) * gain_ref[...]
            ).astype(BF)

    @pl.when(patch < half)
    def _():
        write(low_ref)

    @pl.when(patch >= half)
    def _():
        write(high_ref)


def normed_patches(arrived, picked, norm_gain, patch_count):
    _, length, features = arrived.shape
    per_patch = picked.shape[0] // patch_count
    half = patch_count // 2
    rows = per_patch * length

    def block_spec(i):
        return pl.BlockSpec((1, length, features), lambda p, s: (s[p * per_patch + i], 0, 0))

    return pl.pallas_call(
        norm_kernel,
        grid_spec=pltpu.PrefetchScalarGridSpec(
            num_scalar_prefetch=1,
            grid=(patch_count,),
            in_specs=[block_spec(i) for i in range(per_patch)] + [pl.BlockSpec((1, features), lambda p, s: (0, 0))],
            out_specs=[
                pl.BlockSpec((rows, features), lambda p, s: (jnp.minimum(p, half - 1), 0)),
                pl.BlockSpec((rows, features), lambda p, s: (jnp.maximum(p - half, 0), 0)),
            ],
        ),
        out_shape=[jax.ShapeDtypeStruct((half * rows, features), BF)] * 2,
        compiler_params=params(),
        name="norm",
    )(picked, *([arrived] * per_patch), norm_gain.reshape(1, features))


def nt_dot(a, b):
    return lax.dot_general(a, b, (((1,), (1,)), ((), ())), preferred_element_type=F32)


def squares_of_keys(keys, width):
    features = keys.shape[1]
    head = lax.broadcasted_iota(jnp.int32, (features, 128), 0) // width
    column = lax.broadcasted_iota(jnp.int32, (features, 128), 1)
    member = jnp.where(head == column, 1.0, 0.0).astype(BF)
    squared = jnp.square(keys.astype(F32)).astype(BF)
    return jnp.max(jnp.dot(squared, member, preferred_element_type=F32))


def squares_of_queries(queries, width):
    features, count = queries.shape
    squared = jnp.square(queries.astype(F32)).reshape(features // width, width, count)
    return jnp.max(jnp.sum(squared, axis=1))


def lone_head(pair, which, width):
    kept = pair[which * width : (which + 1) * width]
    blank = jnp.zeros_like(kept)
    return jnp.concatenate([kept, blank] if which == 0 else [blank, kept], axis=0)


def with_ones(values):
    return jnp.concatenate([values, jnp.ones((ONES_ROWS, values.shape[1]), BF)], axis=0)


def plain_head(query_ref, key_ref, value_ref, head, width):
    pair = 2 * width * (head // 2)
    query = lone_head(query_ref[pair : pair + 2 * width, :], head % 2, width)
    total = None
    for at in range(0, key_ref.shape[0], KEY_TILE):
        scores = jnp.dot(key_ref[at : at + KEY_TILE, pair : pair + 2 * width], query, preferred_element_type=F32)
        raised = jnp.exp2(scores).astype(BF)
        values = with_ones(value_ref[head * width : (head + 1) * width, at : at + KEY_TILE])
        part = jnp.dot(values, raised, preferred_element_type=F32)
        total = part if total is None else total + part
    return total


def shifted_heads(query_ref, key_ref, value_ref, width, use):
    head_count = key_ref.shape[1] // width
    tiles = query_ref.shape[1] // QUERY_TILE

    def one(step, carry):
        pair, tile = step // tiles, step % tiles
        features = pl.ds(pl.multiple_of(pair * 2 * width, 2 * width), 2 * width)
        columns = pl.ds(pl.multiple_of(tile * QUERY_TILE, QUERY_TILE), QUERY_TILE)
        queries = query_ref[features, columns]
        keys = key_ref[:, features]
        for which in range(2):
            scores = jnp.dot(keys, lone_head(queries, which, width), preferred_element_type=F32)
            top = jnp.max(scores, axis=0, keepdims=True)
            raised = jnp.exp2(scores - top).astype(BF)
            rows = pl.ds(pl.multiple_of(pair * 2 * width + which * width, width), width)
            sums = jnp.dot(with_ones(value_ref[rows, :]), raised, preferred_element_type=F32)
            use(rows, pair * 2 + which, columns, top, sums)
        return carry

    lax.fori_loop(0, head_count // 2 * tiles, one, 0)


def own_kernel(low_ref, high_ref, wk_ref, wqv_ref, query_ref, total_ref, mass_ref, top_ref, key_s, value_s, *, width):
    patch = pl.program_id(0)
    half = pl.num_programs(0) // 2
    features = wk_ref.shape[0]

    def project(normed_ref):
        normed = normed_ref[...]
        key_s[...] = jnp.dot(normed, wk_ref[...], preferred_element_type=F32).astype(BF)
        both = nt_dot(wqv_ref[...], normed)
        query_ref[...] = (both[:features] * (math.log2(math.e) / math.sqrt(width))).astype(BF)
        value_s[...] = both[features:].astype(BF)

    @pl.when(patch < half)
    def _():
        project(low_ref)

    @pl.when(patch >= half)
    def _():
        project(high_ref)

    bound = squares_of_queries(query_ref[...], width) * squares_of_keys(key_s[...], width)
    small = bound < SAFE_SCORE * SAFE_SCORE

    @pl.when(small)
    def _():
        for head in range(features // width):
            sums = plain_head(query_ref, key_s, value_s, head, width)
            total_ref[head * width : (head + 1) * width, :] = sums[:width]
            mass_ref[head : head + 1, :] = sums[width : width + 1]
        top_ref[...] = jnp.zeros_like(top_ref)

    @pl.when(jnp.logical_not(small))
    def _():
        def use(rows, head, columns, top, sums):
            total_ref[rows, columns] = sums[:width]
            mass_ref[pl.ds(head, 1), columns] = sums[width : width + 1]
            top_ref[pl.ds(head, 1), columns] = top

        shifted_heads(query_ref, key_s, value_s, width, use)


def own_attention(low, high, wk, wqv, patch_count):
    features = wk.shape[0]
    half = patch_count // 2
    rows = low.shape[0] // half
    width = features // HEADS
    whole = lambda p: (0, 0)
    along = lambda p: (0, p)
    return pl.pallas_call(
        functools.partial(own_kernel, width=width),
        grid=(patch_count,),
        in_specs=[
            pl.BlockSpec((rows, features), lambda p: (jnp.minimum(p, half - 1), 0)),
            pl.BlockSpec((rows, features), lambda p: (jnp.maximum(p - half, 0), 0)),
            pl.BlockSpec(wk.shape, whole),
            pl.BlockSpec(wqv.shape, whole),
        ],
        out_specs=[
            pl.BlockSpec((features, rows), along),
            pl.BlockSpec((features, rows), along),
            pl.BlockSpec((HEADS, rows), along),
            pl.BlockSpec((HEADS, rows), along),
        ],
        out_shape=[
            jax.ShapeDtypeStruct((features, patch_count * rows), BF),
            jax.ShapeDtypeStruct((features, patch_count * rows), F32),
            jax.ShapeDtypeStruct((HEADS, patch_count * rows), F32),
            jax.ShapeDtypeStruct((HEADS, patch_count * rows), F32),
        ],
        scratch_shapes=[pltpu.VMEM((rows, features), BF), pltpu.VMEM((features, rows), BF)],
        compiler_params=params(),
        cost_estimate=pl.CostEstimate(flops=40 * 10**9, bytes_accessed=28 * 10**6, transcendentals=0),
        name="own",
    )(low, high, wk, wqv)


def partner_kernel(
    picked_ref,
    source_ref,
    within_ref,
    left_ref,
    low_ref,
    high_ref,
    right_ref,
    query_ref,
    total_ref,
    mass_ref,
    top_ref,
    wk_ref,
    wv_ref,
    wo_ref,
    arrived_ref,
    out_ref,
    normed_s,
    key_s,
    value_s,
    mixed_s,
    *,
    width,
):
    patch = pl.program_id(0)
    features = wk_ref.shape[0]
    for number, normed_ref in enumerate((left_ref, low_ref, high_ref, right_ref)):

        @pl.when(source_ref[patch] == number)
        def _(normed_ref=normed_ref):
            normed_s[...] = normed_ref[...]

    normed = normed_s[...]
    key_s[...] = jnp.dot(normed, wk_ref[...], preferred_element_type=F32).astype(BF)
    value_s[...] = nt_dot(wv_ref[...], normed).astype(BF)
    bound = squares_of_queries(query_ref[...], width) * squares_of_keys(key_s[...], width)
    unshifted = jnp.max(jnp.abs(top_ref[...])) == 0.0
    small = jnp.logical_and(bound < SAFE_SCORE * SAFE_SCORE, unshifted)

    @pl.when(small)
    def _():
        for head in range(features // width):
            sums = plain_head(query_ref, key_s, value_s, head, width)
            rows = slice(head * width, (head + 1) * width)
            mass = mass_ref[head : head + 1, :] + sums[width : width + 1]
            mixed_s[rows, :] = ((total_ref[rows, :] + sums[:width]) / mass).astype(BF)

    @pl.when(jnp.logical_not(small))
    def _():
        def use(rows, head, columns, top, sums):
            one = pl.ds(head, 1)
            before = top_ref[one, columns]
            highest = jnp.maximum(before, top)
            mine, theirs = jnp.exp2(before - highest), jnp.exp2(top - highest)
            mass = mass_ref[one, columns] * mine + sums[width : width + 1] * theirs
            mixed_s[rows, columns] = ((total_ref[rows, columns] * mine + sums[:width] * theirs) / mass).astype(BF)

        shifted_heads(query_ref, key_s, value_s, width, use)

    length = arrived_ref.shape[1]
    per_patch = mixed_s.shape[1] // length
    mixed = lax.dot_general(mixed_s[...], wo_ref[...], (((0,), (0,)), ((), ())), preferred_element_type=F32)
    for i in range(per_patch):
        slot = picked_ref[patch * per_patch + i]
        out_ref[slot] = (arrived_ref[slot].astype(F32) + mixed[i * length : (i + 1) * length]).astype(BF)


def partner_attention(picked, source, within, sets, query, total, mass, top, wk, wv, wo, arrived):
    features = wk.shape[0]
    patch_count = source.shape[0]
    rows = query.shape[1] // patch_count
    whole = lambda p, *s: (0, 0)
    whole3 = lambda p, *s: (0, 0, 0)
    along = lambda p, *s: (0, p)

    def set_spec(number):
        return pl.BlockSpec((rows, features), lambda p, k, s, w: (jnp.where(s[p] == number, w[p], 0), 0))

    return pl.pallas_call(
        functools.partial(partner_kernel, width=features // HEADS),
        grid_spec=pltpu.PrefetchScalarGridSpec(
            num_scalar_prefetch=3,
            grid=(patch_count,),
            in_specs=[set_spec(number) for number in range(4)]
            + [
                pl.BlockSpec((features, rows), along),
                pl.BlockSpec((features, rows), along),
                pl.BlockSpec((HEADS, rows), along),
                pl.BlockSpec((HEADS, rows), along),
                pl.BlockSpec(wk.shape, whole),
                pl.BlockSpec(wv.shape, whole),
                pl.BlockSpec(wo.shape, whole),
                pl.BlockSpec(arrived.shape, whole3),
            ],
            out_specs=pl.BlockSpec(arrived.shape, whole3),
            scratch_shapes=[
                pltpu.VMEM((rows, features), BF),
                pltpu.VMEM((rows, features), BF),
                pltpu.VMEM((features, rows), BF),
                pltpu.VMEM((features, rows), BF),
            ],
        ),
        out_shape=jax.ShapeDtypeStruct(arrived.shape, BF),
        compiler_params=params(),
        cost_estimate=pl.CostEstimate(flops=40 * 10**9, bytes_accessed=28 * 10**6, transcendentals=0),
        name="partner",
    )(picked, source, within, *sets, query, total, mass, top, wk, wv, wo, arrived)


def body(points, order, offsets, norm_gain, w_qkv, w_out):
    features = points.shape[1]
    block_count = order.shape[0]
    block_rows = points.shape[0] // block_count
    patch_count = offsets.shape[0]
    shards = lax.axis_size("seq")
    capacity = (block_count + shards - 1) // shards
    ring = ring_order(shards)
    ring_next = [(ring[e], ring[(e + 1) % shards]) for e in range(shards)]
    ring_before = [(ring[e], ring[e - 1]) for e in range(shards)]
    places = jnp.asarray(ring, jnp.int32)

    block_ids = jnp.arange(block_count, dtype=jnp.int32)
    shard_ids = jnp.arange(shards, dtype=jnp.int32)
    goal = order // block_count
    target = jnp.sum(jnp.where(goal[:, None] == shard_ids[None, :], places[None, :], 0), axis=1)
    local_pos = order % block_count
    earlier = (target[None, :] == target[:, None]) & (block_ids[None, :] < block_ids[:, None])
    slot_pos = target * capacity + jnp.sum(earlier.astype(jnp.int32), axis=1)
    slot_ids = jnp.arange(shards * capacity, dtype=jnp.int32)
    matches = slot_ids[:, None] == slot_pos[None, :]
    source_ids = jnp.sum(jnp.where(matches, block_ids[None, :], 0), axis=1)
    outgoing_pos = jnp.sum(jnp.where(matches, local_pos[None, :] + 1, 0), axis=1) - 1
    told = jnp.concatenate(
        [outgoing_pos.reshape(shards, capacity), jnp.broadcast_to(offsets[None, :], (shards, patch_count))], axis=1
    )
    heard = lax.all_to_all(told, "seq", split_axis=0, concat_axis=0, tiled=True)
    blocks = points.reshape(block_count, block_rows, features)
    outgoing = moved_blocks(blocks, source_ids, "send_order")
    arrived = lax.all_to_all(outgoing, "seq", split_axis=0, concat_axis=0, tiled=True)

    arrived_pos = heard[:, :capacity].reshape(-1)
    my_range = jnp.sum(jnp.where(places == lax.axis_index("seq"), shard_ids, 0))
    my_offsets = jnp.sum(jnp.where(shard_ids[:, None] == my_range, heard[:, capacity:], 0), axis=0)
    picked = jnp.sum(jnp.where(arrived_pos[None, :] == block_ids[:, None], slot_ids[None, :], 0), axis=1)
    where = jnp.arange(patch_count, dtype=jnp.int32) + my_offsets + REACH
    half = patch_count // 2

    low, high = normed_patches(arrived, picked, norm_gain, patch_count)
    left = lax.ppermute(high, "seq", ring_next)
    right = lax.ppermute(low, "seq", ring_before)
    wk = w_qkv[:, features : 2 * features]
    wqv = jnp.concatenate([w_qkv[:, :features], w_qkv[:, 2 * features :]], axis=1).T
    query, total, mass, top = own_attention(low, high, wk, wqv, patch_count)
    returning = partner_attention(
        picked,
        where // half,
        where % half,
        (left, low, high, right),
        query,
        total,
        mass,
        top,
        wk,
        wqv[features:],
        w_out,
        arrived,
    )
    homeward = lax.all_to_all(returning, "seq", split_axis=0, concat_axis=0, tiled=True)
    return moved_blocks(homeward, slot_pos, "home_order").reshape(-1, features)


def solution(mesh):
    return jax.shard_map(
        body,
        mesh=mesh,
        in_specs=(
            P(("scene", "seq"), None),
            P(("scene", "seq")),
            P(("scene", "seq")),
            P(),
            P(),
            P(),
        ),
        out_specs=P(("scene", "seq"), None),
        check_vma=False,
    )
```

time: 993 us -> 700 us (0.70)
  Pallas kernels: 0 us -> 485 us
  waiting for transfers between devices: 502 us -> 86.7 us
  matrix products: 216 us -> 0 us
  local copies, waits for them, and re-layouts: 126 us -> 6.2 us
  other arithmetic: 121 us -> 5.63 us
  blocking collectives: 0 us -> 96.5 us
    pallas_call x0 -> x5, Pallas kernels: none -> 485 us  [the longest x2 258 us: moved_blocks(): pl.pallas_call(kernel, grid_spec=pltpu.PrefetchScalarGridSpec(num_scalar_...]
    ppermute x2, waiting for transfers between devices: 319 us -> 0.01 us  [the longest x1 0.01 us: body(): left = lax.ppermute(high, 'seq', ring_next)]
    dot_general x66 -> x0, matrix products: 216 us -> none  [the longest x32 130 us: attend_one(): jnp.dot(weights, value_block, preferred_element_type=jnp.float32)]
    all_to_all x0 -> x1, blocking collectives: none -> 96.5 us  [body(): lax.all_to_all(returning, 'seq', split_axis=0, concat_axis=0, tiled=True)]
    all_to_all x2 -> x1, waiting for transfers between devices: 91.7 us -> 0.01 us  [body(): heard = lax.all_to_all(told, 'seq', split_axis=0, concat_axis=0, tiled=True)]
    gather x10 -> x0, local copies, waits for them, and re-layouts: 66.9 us -> none  [the longest x5 46.1 us: body(): partner = stacked[:, partner_index]]
    reduce_sum x35 -> x4, other arithmetic: 66.7 us -> 2.28 us  [the longest x1 0.74 us: body(): jnp.sum(jnp.where(goal[:, None] == shard_ids[None, :], places[None, :], 0...]
    concatenate x2 -> x0, other arithmetic: 32.2 us -> none  [the longest x1 24.1 us: body(): stacked = jnp.concatenate([from_left, own_pair, from_right], axis=1)]
  transfers between devices with their start and end apart: 5 -> 4, of which waited for: 4 -> 1; matrix products, arithmetic and copies ran while one was open for 5% -> 1% of each run, Pallas kernels for 0% -> 34%
where the time goes in v1:
time: 700 us; the launch traced here: 697 us
  Pallas kernels  485 us (69%)
  blocking collectives  96.5 us (14%)
  waiting for transfers between devices  86.7 us (12%)
  starting transfers between devices  16.3 us (2%)
    pallas_call x2, Pallas kernels, moved_blocks(): pl.pallas_call(kernel, grid_spec=pltpu.PrefetchScalarGridSpec(num_scalar_...  258 us
    pallas_call x1, Pallas kernels, partner_attention(): pl.pallas_call(functools.partial(partner_kernel, width=features // HEADS)...  113 us
    pallas_call x1, Pallas kernels, own_attention(): pl.pallas_call(functools.partial(own_kernel, width=width), grid=(patch_co...  106 us
    all_to_all x1, blocking collectives, body(): lax.all_to_all(returning, 'seq', split_axis=0, concat_axis=0, tiled=True)  96.5 us
    all_to_all x1, waiting for transfers between devices, body(): lax.all_to_all(outgoing, 'seq', split_axis=0, concat_axis=0, tiled=True)  86.7 us
  transfers between devices with their start and end apart: 4, of which 1 were waited for; matrix products, arithmetic and copies ran while one was open for 1% of the time, Pallas kernels for 34%

profile of v1, /device:TPU:12, one launch (start us, length us, event | category | flops | bytes accessed | tf_op | source)
XLA Modules:
  0.0 696.9 jit_solution(4683779174146314208)
XLA Ops:
  0.0 0.7 fusion.1
  0.7 0.7 select_reduce_fusion.3
  1.4 0.2 convert_reduce_fusion
  1.6 0.0 copy-start.2
  1.6 0.6 select_reduce_fusion
  2.2 0.1 sub.18
  2.3 0.1 copy.22
  2.4 0.7 pad.3.clone
  3.1 0.1 add_bitcast_fusion
  3.2 0.7 copy.23
  3.9 7.2 %all-to-all-start = ((s32[16,1,6]{2,1,0:T(1,128)}), s32[16,1,6]{2,1,0:T(1,128)S(1)}, u32[]{:S(2)}, u32[]{:S(2)}) async-start(s32[16,1,6]{2,1,0:T(1,128)} %copy.23), calls=%async_computation | async-start | bytes 16384 | tf_op jit(solution)/shard_map/all_to_all | solution.py:394
  11.1 129.1 %send_order.1 = bf16[32,128,512]{2,1,0:T(8,128)(2,1)} custom-call(s32[32]{0:T(128)} %get-tuple-element.17.index_ref, bf16[32,128,512]{2,1,0:T(8,128)(2,1)} %bitcast.8), custom_call_target="tpu_custom_call" | custom-call | tf_op jit(solution)/shard_map/send_order/pallas_call | solution.py:55
  140.2 0.0 copy-done.2
  140.2 0.0 copy-start.1
  140.2 0.0 all-to-all-done
  140.2 7.1 %all-to-all-start.1 = ((bf16[32,128,512]{2,1,0:T(8,128)(2,1)}), bf16[32,128,512]{2,1,0:T(8,128)(2,1)}, u32[]{:S(2)}, u32[]{:S(2)}) async-start(bf16[32,128,512]{2,1,0:T(8,128)(2,1)} %send_order.1), calls=%async_computation.1 | async-start | bytes 8388608 | tf_op jit(solution)/shard_map/all_to_all | solution.py:397
  147.3 0.0 copy-done.1
  147.3 1.0 fusion.3
  148.3 0.2 copy.28
  148.5 0.0 copy-start.5
  148.5 0.2 copy.29
  148.7 0.1 maximum_bitcast_fusion.wqv_ref
  148.8 0.0 copy-start
  148.8 1.0 slice.24.wv_ref
  149.8 0.0 copy-done.5
  149.8 0.7 fusion.2
  150.5 0.7 iota_compare_fusion.4
  151.2 0.1 copy.24
  151.3 0.1 copy.25
  151.4 0.1 eq.79
  151.5 0.1 select_reduce_fusion.4
  151.6 0.7 select_reduce_fusion.1.picked_ref
  152.3 0.5 and_select_fusion
  152.8 0.5 and_select_fusion.1.source_ref
  153.3 86.7 %all-to-all-done.1.refs_0_.refs_1_.refs_2_.refs_3_.refs_4_.refs_5_.refs_6_.refs_7_.arrived_ref = bf16[32,128,512]{2,1,0:T(8,128)(2,1)} async-done(((bf16[32,128,512]{2,1,0:T(8,128)(2,1)}), bf16[32,128,512]{2,1,0:T(8,128)(2,1)}, u32[]{:S(2)}, u32[]{:S(2)}) %all-to-all-start.1) | async-done | bytes 4194336 | tf_op jit(solution)/shard_map/all_to_all | solution.py:397
  240.0 7.5 %norm.1 = (bf16[2048,512]{1,0:T(8,128)(2,1)}, bf16[2048,512]{1,0:T(8,128)(2,1)}) custom-call(s32[32]{0:T(128)} %select_reduce_fusion.1.picked_ref, bf16[32,128,512]{2,1,0:T(8,128)(2,1)} %all-to-all-done.1.refs_0_.refs_1_.refs_2_.refs_3_.refs_4_.refs_5_.refs_6_.refs_7_.arrived_ref, ...), custom_call_target="tpu_custom_call" | custom-call | tf_op jit(solution)/shard_map/norm/pallas_call | solution.py:102
  247.5 0.0 copy-done
  247.5 0.1 collective-permute-start
  247.6 2.0 collective-permute-start.1
  249.6 106.4 %own.1 = (bf16[512,4096]{1,0:T(8,128)(2,1)}, f32[512,4096]{1,0:T(8,128)}, f32[8,4096]{1,0:T(8,128)}, f32[8,4096]{1,0:T(8,128)}) custom-call(bf16[2048,512]{1,0:T(8,128)(2,1)} %get-tuple-element.12.low_ref, bf16[2048,512]{1,0:T(8,128)(2,1)} %get-tuple-element.11.high_ref, bf16[512,512]{1,0:T(8,128)(2,1)} %get-tuple-element.22.wk_ref, bf16[1024,512]{1,0:T(8,128)(2,1)} %copy-done), custom_call_target="tpu_custom_call" | custom-call | flops 40000000000 | bytes 28000000 | tf_op jit(solution)/shard_map/own/pallas_call | solution.py:231
  356.0 0.0 collective-permute-done.left_ref
  356.0 0.0 copy-start.3
  356.0 0.0 collective-permute-done.1.right_ref
  356.0 0.0 copy-start.4
  356.0 1.3 copy-done.3
  357.3 0.6 copy-done.4
  357.9 113.1 %partner.1 = bf16[32,128,512]{2,1,0:T(8,128)(2,1)} custom-call(s32[32]{0:T(128)} %select_reduce_fusion.1.picked_ref, s32[4]{0:T(128)} %and_select_fusion.1.source_ref, s32[4]{0:T(128)} %get-tuple-element.19.within_ref, bf16[2048,512]{1,0:T(8,128)(2,1)} %copy-done.3, bf16[2048,512]{1,0:T(8,128)(2,1)} %get-tuple-element.12.low_ref, ...), custom_call_target="tpu_custom_call" | custom-call | flops 40000000000 | bytes 28000000 | tf_op jit(solution)/shard_map/partner/pallas_call | solution.py:337
  471.1 96.5 %all_to_all.22.source_ref = bf16[32,128,512]{2,1,0:T(8,128)(2,1)} all-to-all(bf16[32,128,512]{2,1,0:T(8,128)(2,1)} %partner.1), channel_id=1, replica_groups=mesh['scene'=2,'seq'=16] {'seq'}, dimensions={0} | all-to-all | bytes 8388608 | tf_op jit(solution)/shard_map/all_to_all | solution.py:426
  567.6 129.1 %home_order.1 = bf16[32,128,512]{2,1,0:T(8,128)(2,1)} custom-call(s32[32]{0:T(128)} %copy-done.2, bf16[32,128,512]{2,1,0:T(8,128)(2,1)} %all_to_all.22.source_ref), custom_call_target="tpu_custom_call" | custom-call | tf_op jit(solution)/shard_map/home_order/pallas_call | solution.py:55
  (3 shorter events, 0.0 us)
Async XLA Ops:
  1.6 138.6 %copy-start.2 = (s32[32]{0:T(128)}, s32[32]{0:T(128)S(1)}, u32[]{:S(2)}) copy-start(s32[32]{0:T(128)S(1)} %multiply_add_fusion.index_ref) | copy-start | bytes 388
  3.9 136.3 %all-to-all-start = ((s32[16,1,6]{2,1,0:T(1,128)}), s32[16,1,6]{2,1,0:T(1,128)S(1)}, u32[]{:S(2)}, u32[]{:S(2)}) async-start(s32[16,1,6]{2,1,0:T(1,128)} %copy.23), calls=%async_computation | async-start | bytes 16384 | tf_op jit(solution)/shard_map/all_to_all | solution.py:394
  140.2 7.1 %copy-start.1 = (bf16[512,1536]{1,0:T(8,128)(2,1)S(1)}, bf16[512,1536]{1,0:T(8,128)(2,1)}, u32[]{:S(2)}) copy-start(bf16[512,1536]{1,0:T(8,128)(2,1)} %param.11) | copy-start | bytes 4718596
  140.2 99.8 %all-to-all-start.1 = ((bf16[32,128,512]{2,1,0:T(8,128)(2,1)}), bf16[32,128,512]{2,1,0:T(8,128)(2,1)}, u32[]{:S(2)}, u32[]{:S(2)}) async-start(bf16[32,128,512]{2,1,0:T(8,128)(2,1)} %send_order.1), calls=%async_computation.1 | async-start | bytes 8388608 | tf_op jit(solution)/shard_map/all_to_all | solution.py:397
  148.5 1.3 copy-start.5
  148.8 98.7 %copy-start = (bf16[1024,512]{1,0:T(8,128)(2,1)}, bf16[1024,512]{1,0:T(8,128)(2,1)S(1)}, u32[]{:S(2)}) copy-start(bf16[1024,512]{1,0:T(8,128)(2,1)S(1)} %maximum_bitcast_fusion.wqv_ref) | copy-start | bytes 3145732
  247.5 108.5 %collective-permute-start = (bf16[2048,512]{1,0:T(8,128)(2,1)}, bf16[2048,512]{1,0:T(8,128)(2,1)S(1)}, u32[]{:S(2)}, u32[]{:S(2)}) collective-permute-start(bf16[2048,512]{1,0:T(8,128)(2,1)} %get-tuple-element.11.high_ref), channel_id=1, source_target_pairs={{0,4},{4,8},{8,12},{12,13},{13,9},{9,5},{5,1},{1,3},{3,7},{7,11},{... | collective-permute-start | bytes 6291464 | tf_op jit(solution)/shard_map/ppermute | solution.py:407
  247.6 108.4 %collective-permute-start.1 = (bf16[2048,512]{1,0:T(8,128)(2,1)}, bf16[2048,512]{1,0:T(8,128)(2,1)S(1)}, u32[]{:S(2)}, u32[]{:S(2)}) collective-permute-start(bf16[2048,512]{1,0:T(8,128)(2,1)} %get-tuple-element.12.low_ref), channel_id=1, source_target_pairs={{0,2},{4,0},{8,4},{12,8},{13,12},{9,13},{5,9},{1,5},{3,1},{7,3},{1... | collective-permute-start | bytes 6291464 | tf_op jit(solution)/shard_map/ppermute | solution.py:408
  356.0 1.3 copy-start.3
  356.0 1.9 copy-start.4

commit v2 on v0

v2 whole, which is shorter than its diff:
```python
import functools
import math

import jax
import jax.numpy as jnp
from jax import lax
from jax.experimental import pallas as pl
from jax.experimental.pallas import tpu as pltpu
from jax.sharding import PartitionSpec as P

HEADS = 8
REACH = 2
KEY_TILE = 512
QUERY_TILE = 128
ONES_ROWS = 16
QUARTERS = 8
FIRST = 3
LEAST_MASS = 1e-20
MOST_MASS = 1e30
VMEM_BYTES = 60 * 1024 * 1024
BF = jnp.bfloat16
F32 = jnp.float32


def ring_order(count):
    grids = {16: (4, 2, 2), 64: (4, 4, 4)}
    if count not in grids:
        return list(range(count))
    deep, tall, wide = grids[count]
    columns = [(0, x) for x in range(wide)]
    for y in range(1, tall):
        across = range(wide - 1, 0, -1) if y % 2 else range(1, wide)
        columns += [(y, x) for x in across]
    columns += [(y, 0) for y in range(tall - 1, 0, -1)]
    ring = []
    for at, (y, x) in enumerate(columns):
        along = range(deep) if at % 2 == 0 else range(deep - 1, -1, -1)
        ring += [(z * tall + y) * wide + x for z in along]
    return ring


def params(**more):
    return pltpu.CompilerParams(vmem_limit_bytes=VMEM_BYTES, **more)


def each(count, act):
    def step(i, carry):
        act(i)
        return carry

    lax.fori_loop(0, count, step, 0)


def send_kernel(
    order_ref, offsets_ref, places_ref, points_ref, gain_ref, out_ref, slot_ref, told_ref, points_s, normed_s, taken_s, in_sems, out_sems
):
    block_count, length, features = points_s.shape
    shards = places_ref.shape[0]
    capacity = out_ref.shape[0] // shards
    group = 4

    def copy_in(g):
        rows = pl.ds(g * group, group)
        return pltpu.make_async_copy(points_ref.at[rows], points_s.at[rows], in_sems.at[g])

    def copy_out(b):
        return pltpu.make_async_copy(normed_s.at[b], out_ref.at[slot_ref[b]], out_sems.at[b])

    each(block_count // group, lambda g: copy_in(g).start())

    def clear(d):
        taken_s[d] = 0
        for i in range(capacity):
            told_ref[d * capacity + i] = -1

    each(shards, clear)
    for i in range(offsets_ref.shape[0]):
        told_ref[shards * capacity + i] = offsets_ref[i]

    def place(b):
        position = order_ref[b]
        device = places_ref[lax.div(position, block_count)]
        rank = taken_s[device]
        taken_s[device] = rank + 1
        slot_ref[b] = device * capacity + rank
        told_ref[device * capacity + rank] = lax.rem(position, block_count)

    each(block_count, place)

    def normalise(g):
        copy_in(g).wait()
        values = points_s[pl.ds(g * group, group)].astype(F32).reshape(group * length, features)
        centred = values - jnp.mean(values, axis=-1, keepdims=True)
        spread = jnp.mean(jnp.square(centred), axis=-1, keepdims=True)
        result = (centred * lax.rsqrt(spread + 1e-05) * gain_ref[...]).astype(BF)
        normed_s[pl.ds(g * group, group)] = result.reshape(group, length, features)
        for i in range(group):
            copy_out(g * group + i).start()

    each(block_count // group, normalise)
    each(block_count, lambda b: copy_out(b).wait())


def normed_to_send(blocks, order, offsets, norm_gain, ring, capacity):
    block_count, length, features = blocks.shape
    shards = len(ring)
    return pl.pallas_call(
        send_kernel,
        grid_spec=pltpu.PrefetchScalarGridSpec(
            num_scalar_prefetch=3,
            grid=(1,),
            in_specs=[pl.BlockSpec(memory_space=pl.ANY), pl.BlockSpec((1, features), lambda p, *s: (0, 0))],
            out_specs=[pl.BlockSpec(memory_space=pl.ANY)] + [pl.BlockSpec(memory_space=pltpu.SMEM)] * 2,
            scratch_shapes=[
                pltpu.VMEM(blocks.shape, BF),
                pltpu.VMEM(blocks.shape, BF),
                pltpu.SMEM((shards,), jnp.int32),
                pltpu.SemaphoreType.DMA((block_count // 4,)),
                pltpu.SemaphoreType.DMA((block_count,)),
            ],
        ),
        out_shape=[
            jax.ShapeDtypeStruct((shards * capacity, length, features), BF),
            jax.ShapeDtypeStruct((block_count,), jnp.int32),
            jax.ShapeDtypeStruct((shards * capacity + offsets.shape[0],), jnp.int32),
        ],
        compiler_params=params(),
        name="send",
    )(order, offsets, jnp.asarray(ring, jnp.int32), blocks, norm_gain.reshape(1, features))


def sort_kernel(
    known_ref, here_ref, arrived_ref, low_ref, high_ref, picked_ref, set_ref, within_ref, held_s, in_sems, out_sems
):
    patch_count, _, per_patch = held_s.shape[:3]
    half = patch_count // 2
    slot_count = arrived_ref.shape[0]
    entry = slot_count + patch_count
    capacity = slot_count // (known_ref.shape[0] // entry)
    my_place, my_range = here_ref[0], here_ref[1]

    def copy_in(patch, i):
        at = patch * per_patch + i
        return pltpu.make_async_copy(arrived_ref.at[picked_ref[at]], held_s.at[patch, :, i], in_sems.at[at])

    def copy_out(patch):
        out_ref = low_ref if patch < half else high_ref
        return pltpu.make_async_copy(held_s.at[patch], out_ref.at[patch % half], out_sems.at[patch])

    each(patch_count * per_patch, lambda i: picked_ref.__setitem__(i, 0))

    def find(sender):
        for rank in range(capacity):
            position = known_ref[sender * entry + my_place * capacity + rank]

            @pl.when(position >= 0)
            def _():
                picked_ref[position] = sender * capacity + rank

    each(slot_count // capacity, find)
    for patch in range(patch_count):
        for i in range(per_patch):
            copy_in(patch, i).start()
    for patch in range(patch_count):
        wanted = patch + known_ref[my_range * entry + slot_count + patch] + REACH
        set_ref[patch] = lax.div(wanted, half)
        within_ref[patch] = lax.rem(wanted, half)
    for patch in range(patch_count):
        for i in range(per_patch):
            copy_in(patch, i).wait()
        copy_out(patch).start()
    for patch in range(patch_count):
        copy_out(patch).wait()


def sorted_patches(arrived, known, here, block_count, patch_count):
    _, quarters, length, features = arrived.shape
    per_patch = block_count // patch_count
    half = patch_count // 2
    patch_shape = (quarters, per_patch, length, features)
    counts = (block_count, patch_count, patch_count)
    low, high, *found = pl.pallas_call(
        sort_kernel,
        grid_spec=pltpu.PrefetchScalarGridSpec(
            num_scalar_prefetch=2,
            grid=(1,),
            in_specs=[pl.BlockSpec(memory_space=pl.ANY)],
            out_specs=[pl.BlockSpec(memory_space=pl.ANY)] * 2 + [pl.BlockSpec(memory_space=pltpu.SMEM)] * 3,
            scratch_shapes=[
                pltpu.VMEM((patch_count,) + patch_shape, BF),
                pltpu.SemaphoreType.DMA((block_count,)),
                pltpu.SemaphoreType.DMA((patch_count,)),
            ],
        ),
        out_shape=[jax.ShapeDtypeStruct((half,) + patch_shape, BF)] * 2
        + [jax.ShapeDtypeStruct((count,), jnp.int32) for count in counts],
        compiler_params=params(),
        name="sort",
    )(known, here, arrived)
    return low.reshape(-1, features), high.reshape(-1, features), *found


def home_kernel(slot_ref, points_ref, first_ref, rest_ref, out_ref, points_s, first_s, rest_s, out_s, in_sems, out_sems):
    block_count = points_s.shape[0]
    group = block_count // out_sems.shape[0]

    def copies_in(g):
        rows = pl.ds(g * group, group)
        sems = in_sems.at[g]
        yield pltpu.make_async_copy(points_ref.at[rows], points_s.at[rows], sems.at[0])
        for i in range(group):
            b = g * group + i
            yield pltpu.make_async_copy(first_ref.at[slot_ref[b]], first_s.at[b], sems.at[1 + i])
            yield pltpu.make_async_copy(rest_ref.at[slot_ref[b]], rest_s.at[b], sems.at[1 + group + i])

    def copy_out(g):
        rows = pl.ds(g * group, group)
        return pltpu.make_async_copy(out_s.at[rows], out_ref.at[rows], out_sems.at[g])

    def begin(g):
        for copy in copies_in(g):
            copy.start()

    def add(g):
        for copy in copies_in(g):
            copy.wait()
        rows = pl.ds(g * group, group)
        out_s[rows, :FIRST] = (points_s[rows, :FIRST].astype(F32) + first_s[rows].astype(F32)).astype(BF)
        out_s[rows, FIRST:] = (points_s[rows, FIRST:].astype(F32) + rest_s[rows].astype(F32)).astype(BF)
        copy_out(g).start()

    each(block_count // group, begin)
    each(block_count // group, add)
    each(block_count // group, lambda g: copy_out(g).wait())


def home_sum(blocks, first, rest, slots):
    block_count = blocks.shape[0]
    group = 4
    return pl.pallas_call(
        home_kernel,
        grid_spec=pltpu.PrefetchScalarGridSpec(
            num_scalar_prefetch=1,
            grid=(1,),
            in_specs=[pl.BlockSpec(memory_space=pl.ANY)] * 3,
            out_specs=pl.BlockSpec(memory_space=pl.ANY),
            scratch_shapes=[
                pltpu.VMEM(blocks.shape, BF),
                pltpu.VMEM((block_count,) + first.shape[1:], BF),
                pltpu.VMEM((block_count,) + rest.shape[1:], BF),
                pltpu.VMEM(blocks.shape, BF),
                pltpu.SemaphoreType.DMA((block_count // group, 1 + 2 * group)),
                pltpu.SemaphoreType.DMA((block_count // group,)),
            ],
        ),
        out_shape=jax.ShapeDtypeStruct(blocks.shape, BF),
        compiler_params=params(),
        name="home",
    )(slots, blocks, first, rest)


def nt_dot(a, b):
    return lax.dot_general(a, b, (((1,), (1,)), ((), ())), preferred_element_type=F32)


def in_range(mass):
    good = jnp.logical_and(mass >= LEAST_MASS, mass <= MOST_MASS)
    return jnp.min(jnp.where(good, 1.0, 0.0)) > 0.5


def lone_head(pair, which, width):
    kept = pair[which * width : (which + 1) * width]
    blank = jnp.zeros_like(kept)
    return jnp.concatenate([kept, blank] if which == 0 else [blank, kept], axis=0)


def with_ones(values):
    return jnp.concatenate([values, jnp.ones((ONES_ROWS, values.shape[1]), BF)], axis=0)


def plain_head(query_ref, key_ref, value_ref, head, width):
    pair = 2 * width * (head // 2)
    query = lone_head(query_ref[pair : pair + 2 * width, :], head % 2, width)
    total = None
    for at in range(0, key_ref.shape[0], KEY_TILE):
        scores = jnp.dot(key_ref[at : at + KEY_TILE, pair : pair + 2 * width], query, preferred_element_type=F32)
        raised = jnp.exp(scores).astype(BF)
        values = with_ones(value_ref[head * width : (head + 1) * width, at : at + KEY_TILE])
        part = jnp.dot(values, raised, preferred_element_type=F32)
        total = part if total is None else total + part
    return total


def shifted_heads(query_ref, key_ref, value_ref, width, use):
    tiles = query_ref.shape[1] // QUERY_TILE

    def one(tile):
        columns = pl.ds(pl.multiple_of(tile * QUERY_TILE, QUERY_TILE), QUERY_TILE)
        for head in range(key_ref.shape[1] // width):
            pair = 2 * width * (head // 2)
            features = slice(pair, pair + 2 * width)
            query = lone_head(query_ref[features, columns], head % 2, width)
            scores = jnp.dot(key_ref[:, features], query, preferred_element_type=F32)
            top = jnp.max(scores, axis=0, keepdims=True)
            raised = jnp.exp(scores - top).astype(BF)
            rows = slice(head * width, (head + 1) * width)
            sums = jnp.dot(with_ones(value_ref[rows, :]), raised, preferred_element_type=F32)
            use(rows, head, columns, top, sums)

    each(tiles, one)


def parts_of(columns):
    first = columns * FIRST // QUARTERS
    return (slice(0, first), slice(first, columns))


def own_kernel(low_ref, high_ref, wk_ref, wqv_ref, *refs, width):
    *out_refs, query_s, key_s, value_s, total_s, mass_s, top_s = refs
    patch = pl.program_id(0)
    half = pl.num_programs(0) // 2
    features = wk_ref.shape[0]
    parts = [(columns, out_refs[4 * i : 4 * i + 4]) for i, columns in enumerate(parts_of(query_s.shape[1]))]

    def project(normed_ref):
        normed = normed_ref[...]
        key_s[...] = jnp.dot(normed, wk_ref[...], preferred_element_type=F32).astype(BF)
        both = nt_dot(wqv_ref[...], normed)
        query_s[...] = both[:features].astype(BF) * (1 / math.sqrt(width))
        value_s[...] = both[features:].astype(BF)

    @pl.when(patch < half)
    def _():
        project(low_ref)

    @pl.when(patch >= half)
    def _():
        project(high_ref)

    for columns, (query_ref, _, _, _) in parts:
        query_ref[...] = query_s[:, columns]
    masses = []
    for head in range(features // width):
        sums = plain_head(query_s, key_s, value_s, head, width)
        masses.append(sums[width : width + 1])
        for columns, (_, total_ref, mass_ref, _) in parts:
            total_ref[head * width : (head + 1) * width, :] = sums[:width, columns]
            mass_ref[head : head + 1, :] = sums[width : width + 1, columns]
    for _, (_, _, _, top_ref) in parts:
        top_ref[...] = jnp.zeros_like(top_ref)
    small = in_range(jnp.concatenate(masses, axis=0))

    @pl.when(jnp.logical_not(small))
    def _():
        def use(rows, head, columns, top, sums):
            total_s[rows, columns] = sums[:width]
            mass_s[slice(head, head + 1), columns] = sums[width : width + 1]
            top_s[slice(head, head + 1), columns] = top

        shifted_heads(query_s, key_s, value_s, width, use)
        for columns, (_, total_ref, mass_ref, top_ref) in parts:
            total_ref[...] = total_s[:, columns]
            mass_ref[...] = mass_s[:, columns]
            top_ref[...] = top_s[:, columns]


def own_attention(low, high, wk, wqv, patch_count):
    features = wk.shape[0]
    half = patch_count // 2
    rows = low.shape[0] // half
    width = features // HEADS
    whole = lambda p: (0, 0)
    along = lambda p: (0, p)
    specs, shapes = [], []
    for columns in parts_of(rows):
        count = columns.stop - columns.start
        for height, dtype in ((features, BF), (features, F32), (HEADS, F32), (HEADS, F32)):
            specs.append(pl.BlockSpec((height, count), along))
            shapes.append(jax.ShapeDtypeStruct((height, patch_count * count), dtype))
    results = pl.pallas_call(
        functools.partial(own_kernel, width=width),
        grid=(patch_count,),
        in_specs=[
            pl.BlockSpec((rows, features), lambda p: (jnp.minimum(p, half - 1), 0)),
            pl.BlockSpec((rows, features), lambda p: (jnp.maximum(p - half, 0), 0)),
            pl.BlockSpec(wk.shape, whole),
            pl.BlockSpec(wqv.shape, whole),
        ],
        out_specs=specs,
        out_shape=shapes,
        scratch_shapes=[
            pltpu.VMEM((features, rows), BF),
            pltpu.VMEM((rows, features), BF),
            pltpu.VMEM((features, rows), BF),
            pltpu.VMEM((features, rows), F32),
            pltpu.VMEM((HEADS, rows), F32),
            pltpu.VMEM((HEADS, rows), F32),
        ],
        compiler_params=params(),
        cost_estimate=pl.CostEstimate(flops=40 * 10**9, bytes_accessed=28 * 10**6, transcendentals=0),
        name="own",
    )(low, high, wk, wqv)
    return results[:4], results[4:]


def attend_partner(picked_ref, query_ref, total_ref, mass_ref, top_ref, key_ref, value_ref, wo_ref, out_ref, mixed_s):
    patch = pl.program_id(0)
    width = wo_ref.shape[0] // HEADS
    _, quarters, length, _ = out_ref.shape
    per_patch = mixed_s.shape[1] // (quarters * length)

    def finish():
        mixed = lax.dot_general(mixed_s[...], wo_ref[...], (((0,), (0,)), ((), ())), preferred_element_type=F32)
        mixed = mixed.astype(BF)
        for i in range(per_patch):
            slot = picked_ref[patch * per_patch + i]
            for quarter in range(quarters):
                at = (quarter * per_patch + i) * length
                out_ref[slot, quarter] = mixed[at : at + length]

    masses = []
    for head in range(HEADS):
        sums = plain_head(query_ref, key_ref, value_ref, head, width)
        rows = slice(head * width, (head + 1) * width)
        masses.append(mass_ref[head : head + 1, :] + sums[width : width + 1])
        mixed_s[rows, :] = ((total_ref[rows, :] + sums[:width]) * (1.0 / masses[-1])).astype(BF)
    unshifted = jnp.max(jnp.abs(top_ref[...])) == 0.0
    small = jnp.logical_and(in_range(jnp.concatenate(masses, axis=0)), unshifted)
    finish()

    @pl.when(jnp.logical_not(small))
    def _():
        def use(rows, head, columns, top, sums):
            one = slice(head, head + 1)
            before = top_ref[one, columns]
            highest = jnp.maximum(before, top)
            mine, theirs = jnp.exp(before - highest), jnp.exp(top - highest)
            mass = mass_ref[one, columns] * mine + sums[width : width + 1] * theirs
            mixed_s[rows, columns] = ((total_ref[rows, columns] * mine + sums[:width] * theirs) / mass).astype(BF)

        shifted_heads(query_ref, key_ref, value_ref, width, use)
        finish()


def first_kernel(picked_ref, source_ref, within_ref, left_ref, low_ref, high_ref, right_ref, *refs):
    *between, wk_ref, wv_ref, wo_ref, out_ref, key_ref, value_ref, normed_s, mixed_s, sems = refs
    patch = pl.program_id(0)
    rows = normed_s.shape[1]
    now = lax.rem(patch, 2)

    def copy(number, which, at):
        return pltpu.make_async_copy(number.at[pl.ds(which * rows, rows)], normed_s.at[at], sems.at[at])

    def begin(which):
        for number, normed_ref in enumerate((left_ref, low_ref, high_ref, right_ref)):

            @pl.when(source_ref[which] == number)
            def _(normed_ref=normed_ref):
                copy(normed_ref, within_ref[which], lax.rem(which, 2)).start()

    @pl.when(patch == 0)
    def _():
        begin(patch)

    @pl.when(patch + 1 < pl.num_programs(0))
    def _():
        begin(patch + 1)

    copy(low_ref, 0, now).wait()
    normed = normed_s[now]
    key_ref[...] = jnp.dot(normed, wk_ref[...], preferred_element_type=F32).astype(BF)
    value_ref[...] = nt_dot(wv_ref[...], normed).astype(BF)
    attend_partner(picked_ref, *between, key_ref, value_ref, wo_ref, out_ref, mixed_s)


def rest_kernel(picked_ref, *refs):
    attend_partner(picked_ref, *refs)


def own_specs(own, patch_count):
    return [pl.BlockSpec((part.shape[0], part.shape[1] // patch_count), lambda p, *s: (0, p)) for part in own]


def partner_first(picked, source, within, sets, own, wk, wqv, wo, out_shape):
    features = wk.shape[0]
    patch_count = source.shape[0]
    rows = sets[0].shape[0] // (patch_count // 2)
    whole = lambda p, *s: (0, 0)
    below = lambda p, *s: (1, 0)

    return pl.pallas_call(
        first_kernel,
        grid_spec=pltpu.PrefetchScalarGridSpec(
            num_scalar_prefetch=3,
            grid=(patch_count,),
            in_specs=[pl.BlockSpec(memory_space=pl.ANY)] * 4
            + own_specs(own, patch_count)
            + [pl.BlockSpec(wk.shape, whole), pl.BlockSpec(wk.shape, below), pl.BlockSpec(wo.shape, whole)],
            out_specs=[
                pl.BlockSpec(out_shape, lambda p, *s: (0, 0, 0, 0)),
                pl.BlockSpec((rows, features), lambda p, *s: (p, 0)),
                pl.BlockSpec((features, rows), lambda p, *s: (0, p)),
            ],
            scratch_shapes=[
                pltpu.VMEM((2, rows, features), BF),
                pltpu.VMEM((features, own[0].shape[1] // patch_count), BF),
                pltpu.SemaphoreType.DMA((2,)),
            ],
        ),
        out_shape=[
            jax.ShapeDtypeStruct(out_shape, BF),
            jax.ShapeDtypeStruct((patch_count * rows, features), BF),
            jax.ShapeDtypeStruct((features, patch_count * rows), BF),
        ],
        compiler_params=params(),
        cost_estimate=pl.CostEstimate(flops=15 * 10**9, bytes_accessed=28 * 10**6, transcendentals=0),
        name="partner_first",
    )(picked, source, within, *sets, *own, wk, wqv, wo)


def partner_rest(picked, own, keys, values, wo, out_shape, patch_count):
    features = wo.shape[0]
    rows = keys.shape[0] // patch_count
    return pl.pallas_call(
        rest_kernel,
        grid_spec=pltpu.PrefetchScalarGridSpec(
            num_scalar_prefetch=1,
            grid=(patch_count,),
            in_specs=own_specs(own, patch_count)
            + [
                pl.BlockSpec((rows, features), lambda p, *s: (p, 0)),
                pl.BlockSpec((features, rows), lambda p, *s: (0, p)),
                pl.BlockSpec(wo.shape, lambda p, *s: (0, 0)),
            ],
            out_specs=pl.BlockSpec(out_shape, lambda p, *s: (0, 0, 0, 0)),
            scratch_shapes=[pltpu.VMEM((features, own[0].shape[1] // patch_count), BF)],
        ),
        out_shape=jax.ShapeDtypeStruct(out_shape, BF),
        compiler_params=params(),
        cost_estimate=pl.CostEstimate(flops=30 * 10**9, bytes_accessed=28 * 10**6, transcendentals=0),
        name="partner_rest",
    )(picked, *own, keys, values, wo)


def exchanged(value):
    return lax.all_to_all(value, "seq", split_axis=0, concat_axis=0, tiled=True)


def body(points, order, offsets, norm_gain, w_qkv, w_out):
    features = points.shape[1]
    block_count = order.shape[0]
    block_rows = points.shape[0] // block_count
    patch_count = offsets.shape[0]
    shards = lax.axis_size("seq")
    capacity = (block_count + shards - 1) // shards
    ring = ring_order(shards)
    ring_next = [(ring[e], ring[(e + 1) % shards]) for e in range(shards)]
    ring_before = [(ring[e], ring[e - 1]) for e in range(shards)]
    me = lax.axis_index("seq")
    ranges = [ring.index(place) for place in range(shards)]
    here = lax.dynamic_slice(jnp.asarray(list(enumerate(ranges)), jnp.int32), (me, 0), (1, 2)).reshape(2)

    blocks = points.reshape(block_count, block_rows, features)
    outgoing, slots, told = normed_to_send(blocks, order, offsets, norm_gain, ring, capacity)
    arrived = exchanged(outgoing).reshape(-1, QUARTERS, block_rows // QUARTERS, features)
    known = lax.all_gather(told, "seq", tiled=True)
    low, high, picked, source, within = sorted_patches(arrived, known, here, block_count, patch_count)
    left = lax.ppermute(high, "seq", ring_next)
    right = lax.ppermute(low, "seq", ring_before)
    wk = w_qkv[:, features : 2 * features]
    wqv = jnp.concatenate([w_qkv[:, :features], w_qkv[:, 2 * features :]], axis=1).T
    own_first, own_rest = own_attention(low, high, wk, wqv, patch_count)
    slot_shape = arrived.shape[:1], arrived.shape[2:]
    first, keys, values = partner_first(
        picked,
        source,
        within,
        (left, low, high, right),
        own_first,
        wk,
        wqv,
        w_out,
        slot_shape[0] + (FIRST,) + slot_shape[1],
    )
    first_home = exchanged(first)
    rest = partner_rest(
        picked, own_rest, keys, values, w_out, slot_shape[0] + (QUARTERS - FIRST,) + slot_shape[1], patch_count
    )
    rest_home = exchanged(rest)
    split_blocks = blocks.reshape(block_count, QUARTERS, block_rows // QUARTERS, features)
    return home_sum(split_blocks, first_home, rest_home, slots).reshape(-1, features)


def solution(mesh):
    return jax.shard_map(
        body,
        mesh=mesh,
        in_specs=(
            P(("scene", "seq"), None),
            P(("scene", "seq")),
            P(("scene", "seq")),
            P(),
            P(),
            P(),
        ),
        out_specs=P(("scene", "seq"), None),
        check_vma=False,
    )
```

time: 993 us -> 504 us (0.51)
  waiting for transfers between devices: 502 us -> 1.41 us
  Pallas kernels: 0 us -> 324 us
  matrix products: 216 us -> 0 us
  blocking collectives: 0 us -> 151 us
  local copies, waits for them, and re-layouts: 126 us -> 4.93 us
  other arithmetic: 121 us -> 1.05 us
    pallas_call x0 -> x6, Pallas kernels: none -> 324 us  [the longest x1 145 us: own_attention(): pl.pallas_call(functools.partial(own_kernel, width=width), grid=(patch_co...]
    ppermute x2, waiting for transfers between devices: 319 us -> 0.01 us  [the longest x1 0.01 us: body(): right = lax.ppermute(low, 'seq', ring_before)]
    dot_general x66 -> x0, matrix products: 216 us -> none  [the longest x32 130 us: attend_one(): jnp.dot(weights, value_block, preferred_element_type=jnp.float32)]
    all_to_all x3 -> x2, waiting for transfers between devices: 183 us -> 1.41 us  [exchanged(): return lax.all_to_all(value, 'seq', split_axis=0, concat_axis=0, tiled=True)]
    unnamed x0 -> x1, blocking collectives: none -> 87.6 us
    reduce_sum x37 -> x0, other arithmetic: 67 us -> none  [the longest x32 61.9 us: attend_one(): jnp.sum(raised, axis=-1, keepdims=True)]
    gather x10 -> x0, local copies, waits for them, and re-layouts: 66.9 us -> none  [the longest x5 46.1 us: body(): partner = stacked[:, partner_index]]
    all_to_all x0 -> x1, blocking collectives: none -> 63.8 us  [exchanged(): return lax.all_to_all(value, 'seq', split_axis=0, concat_axis=0, tiled=True)]
  transfers between devices with their start and end apart: 5 -> 4, of which waited for: 4 -> 1; matrix products, arithmetic and copies ran while one was open for 5% -> 1% of each run, Pallas kernels for 0% -> 47%
where the time goes in v2:
time: 504 us; the launch traced here: 501 us
  Pallas kernels  324 us (64%)
  blocking collectives  151 us (30%)
  starting transfers between devices  18 us (4%)
    pallas_call x1, Pallas kernels, own_attention(): pl.pallas_call(functools.partial(own_kernel, width=width), grid=(patch_co...  145 us
    pallas_call x1, Pallas kernels, partner_rest(): pl.pallas_call(rest_kernel, grid_spec=pltpu.PrefetchScalarGridSpec(num_sc...  93.2 us
    unnamed x1, blocking collectives  87.6 us
    pallas_call x1, Pallas kernels, partner_first(): pl.pallas_call(first_kernel, grid_spec=pltpu.PrefetchScalarGridSpec(num_s...  67 us
    all_to_all x1, blocking collectives, exchanged(): return lax.all_to_all(value, 'seq', split_axis=0, concat_axis=0, tiled=True)  63.8 us
    all_to_all x2, starting transfers between devices, exchanged(): return lax.all_to_all(value, 'seq', split_axis=0, concat_axis=0, tiled=True)  13.2 us
  transfers between devices with their start and end apart: 4, of which 1 were waited for; matrix products, arithmetic and copies ran while one was open for 1% of the time, Pallas kernels for 47%

profile of v2, /device:TPU:12, one launch (start us, length us, event | category | flops | bytes accessed | tf_op | source)
XLA Modules:
  0.0 501.5 jit_solution(10773361605628319052)
XLA Ops:
  0.0 6.6 %send.1 = (bf16[32,128,512]{2,1,0:T(8,128)(2,1)}, s32[32]{0:T(128)}, s32[36]{0:T(128)}) custom-call(s32[32]{0:T(128)} %order_ref.1, s32[4]{0:T(128)} %offsets_ref.1, s32[16]{0:T(128)} %constant.13.clone.places_ref, bf16[32,128,512]{2,1,0:T(8,128)(2,1)} %bitcast.12, f32[1,512]{1,0:T(1,128)} %bitcast.14), custom_call_target="tpu_custom_call" | custom-call | tf_op jit(solution)/shard_map/send/pallas_call | solution.py:107
  6.7 0.0 copy-start.1
  6.7 7.3 %all-to-all-start = ((bf16[32,128,512]{2,1,0:T(8,128)(2,1)}), bf16[32,128,512]{2,1,0:T(8,128)(2,1)}, u32[]{:S(2)}, u32[]{:S(2)}) async-start(bf16[32,128,512]{2,1,0:T(8,128)(2,1)} %get-tuple-element.26), calls=%async_computation | async-start | bytes 8388608 | tf_op jit(solution)/shard_map/all_to_all | solution.py:546
  14.0 0.0 copy-done.1
  14.0 0.0 copy-start.4
  14.0 0.0 copy-start.3
  14.0 1.0 fusion
  15.0 0.2 copy.11
  15.2 0.2 copy.12
  15.4 0.0 copy-done.4
  15.4 0.7 dynamic-slice
  16.7 0.0 copy-done.3
  16.7 0.2 dynamic-update-slice
  17.0 87.6 %all-reduce.known_ref = s32[576]{0:T(1024)} all-reduce(s32[576]{0:T(1024)S(1)} %dynamic-update-slice), channel_id=1, replica_groups=mesh['scene'=2,'seq'=16] {'seq'}, use_global_device_ids=true, to_apply=%add | all-reduce | flops 576 | bytes 4608
  104.6 1.3 dynamic-slice_bitcast_fusion.here_ref
  105.9 1.0 maximum_bitcast_fusion.wqv_ref.refs_5_
  106.9 1.4 all-to-all-done
  108.3 5.2 %sort.1 = (bf16[2,8,8,16,512]{4,3,2,1,0:T(8,128)(2,1)}, bf16[2,8,8,16,512]{4,3,2,1,0:T(8,128)(2,1)}, s32[32]{0:T(128)}, s32[4]{0:T(128)}, s32[4]{0:T(128)}) custom-call(s32[576]{0:T(1024)} %all-reduce.known_ref, s32[2]{0:T(128)} %dynamic-slice_bitcast_fusion.here_ref, bf16[32,8,16,512]{3,2,1,0:T(8,128)(2,1)} %bitcast.5.arrived_ref), custom_call_target="tpu_custom_call" | custom-call | tf_op jit(solution)/shard_map/sort/pallas_call | solution.py:182
  113.5 4.8 collective-permute-start
  118.4 0.0 collective-permute-start.1
  118.4 145.0 %own.1 = (bf16[512,1536]{1,0:T(8,128)(2,1)}, f32[512,1536]{1,0:T(8,128)}, f32[8,1536]{1,0:T(8,128)}, f32[8,1536]{1,0:T(8,128)}, bf16[512,2560]{1,0:T(8,128)(2,1)...) custom-call(bf16[2048,512]{1,0:T(8,128)(2,1)} %bitcast.16, bf16[2048,512]{1,0:T(8,128)(2,1)} %bitcast.19, ...), custom_call_target="tpu_custom_call" | custom-call | flops 40000000000 | bytes 28000000 | tf_op jit(solution)/shard_map/own/pallas_call | solution.py:380
  263.4 0.0 collective-permute-done.left_ref
  263.4 0.0 copy-start.2
  263.4 0.0 collective-permute-done.1.right_ref
  263.4 1.4 copy-done.2
  264.7 67.0 %partner_first.1 = (bf16[32,3,16,512]{3,2,1,0:T(8,128)(2,1)}, bf16[4096,512]{1,0:T(8,128)(2,1)}, bf16[512,4096]{1,0:T(8,128)(2,1)}) custom-call(s32[32]{0:T(128)} %get-tuple-element.27.picked_ref, s32[4]{0:T(128)} %get-tuple-element.28.source_ref, s32[4]{0:T(128)} %get-tuple-element.29.within_ref, bf16[2048,512]{1,0:T(8,128)(2,1)} %copy-done.2, ...), custom_call_target="tpu_custom_call" | custom-call | flops 15000000512 | bytes 28000000 | tf_op jit(solution)/shard_map/partner_first/pallas_call | solution.py:491
  331.8 5.9 %all-to-all-start.1 = ((bf16[32,3,16,512]{3,2,1,0:T(8,128)(2,1)}), bf16[32,3,16,512]{3,2,1,0:T(8,128)(2,1)S(1)}, u32[]{:S(2)}, u32[]{:S(2)}) async-start(bf16[32,3,16,512]{3,2,1,0:T(8,128)(2,1)} %get-tuple-element.36), calls=%async_computation.1 | async-start | bytes 3145728 | tf_op jit(solution)/shard_map/all_to_all | solution.py:546
  337.6 93.2 %partner_rest.1 = bf16[32,5,16,512]{3,2,1,0:T(8,128)(2,1)} custom-call(s32[32]{0:T(128)} %get-tuple-element.27.picked_ref, bf16[512,2560]{1,0:T(8,128)(2,1)} %get-tuple-element.37.refs_0_, f32[512,2560]{1,0:T(8,128)} %get-tuple-element.38.refs_1_, f32[8,2560]{1,0:T(8,128)} %get-tuple-element.39.refs_2_, f32[8,2560]{1,0:T(8,128)} %get-tuple-element.40.refs_3_, ...), custom_call_target="tpu_custom_call" | custom-call | flops 30000001024 | bytes 28000000 | tf_op jit(solution)/shard_map/partner_rest/pallas_call | solution.py:524
  430.8 0.0 all-to-all-done.1.first_ref
  430.8 0.0 copy-start
  430.8 63.8 %all_to_all.15.rest_ref = bf16[32,5,16,512]{3,2,1,0:T(8,128)(2,1)} all-to-all(bf16[32,5,16,512]{3,2,1,0:T(8,128)(2,1)} %partner_rest.1), channel_id=1, replica_groups=mesh['scene'=2,'seq'=16] {'seq'}, dimensions={0} | all-to-all | bytes 5242880 | tf_op jit(solution)/shard_map/all_to_all | solution.py:546
  494.6 0.0 copy-done
  494.6 6.6 %home.1 = bf16[32,8,16,512]{3,2,1,0:T(8,128)(2,1)} custom-call(s32[32]{0:T(128)} %get-tuple-element.24.slot_ref, bf16[32,8,16,512]{3,2,1,0:T(8,128)(2,1)} %bitcast.13, bf16[32,3,16,512]{3,2,1,0:T(8,128)(2,1)} %copy-done, bf16[32,5,16,512]{3,2,1,0:T(8,128)(2,1)} %all_to_all.15.rest_ref), custom_call_target="tpu_custom_call" | custom-call | tf_op jit(solution)/shard_map/home/pallas_call | solution.py:240
  (1 shorter events, 0.0 us)
Async XLA Ops:
  6.7 7.3 %copy-start.1 = (bf16[512,1536]{1,0:T(8,128)(2,1)S(1)}, bf16[512,1536]{1,0:T(8,128)(2,1)}, u32[]{:S(2)}) copy-start(bf16[512,1536]{1,0:T(8,128)(2,1)} %param.12) | copy-start | bytes 4718596
  6.7 101.7 %all-to-all-start = ((bf16[32,128,512]{2,1,0:T(8,128)(2,1)}), bf16[32,128,512]{2,1,0:T(8,128)(2,1)}, u32[]{:S(2)}, u32[]{:S(2)}) async-start(bf16[32,128,512]{2,1,0:T(8,128)(2,1)} %get-tuple-element.26), calls=%async_computation | async-start | bytes 8388608 | tf_op jit(solution)/shard_map/all_to_all | solution.py:546
  14.0 1.4 copy-start.4
  14.0 2.7 copy-start.3
  113.5 149.8 %collective-permute-start = (bf16[2048,512]{1,0:T(8,128)(2,1)}, bf16[2048,512]{1,0:T(8,128)(2,1)S(1)}, u32[]{:S(2)}, u32[]{:S(2)}) collective-permute-start(bf16[2048,512]{1,0:T(8,128)(2,1)} %bitcast.18), channel_id=1, source_target_pairs={{0,4},{4,8},{8,12},{12,13},{13,9},{9,5},{5,1},{1,3},{3,7},{7,11},{... | collective-permute-start | bytes 6291464 | tf_op jit(solution)/shard_map/ppermute | solution.py:568
  118.4 145.0 %collective-permute-start.1 = (bf16[2048,512]{1,0:T(8,128)(2,1)}, bf16[2048,512]{1,0:T(8,128)(2,1)}, u32[]{:S(2)}, u32[]{:S(2)}) collective-permute-start(bf16[2048,512]{1,0:T(8,128)(2,1)} %bitcast.15), channel_id=1, source_target_pairs={{0,2},{4,0},{8,4},{12,8},{13,12},{9,13},{5,9},{1,5},{3,1},{7,3},{1... | collective-permute-start | bytes 6291464 | tf_op jit(solution)/shard_map/ppermute | solution.py:569
  263.4 1.4 copy-start.2
  331.8 99.1 %all-to-all-start.1 = ((bf16[32,3,16,512]{3,2,1,0:T(8,128)(2,1)}), bf16[32,3,16,512]{3,2,1,0:T(8,128)(2,1)S(1)}, u32[]{:S(2)}, u32[]{:S(2)}) async-start(bf16[32,3,16,512]{3,2,1,0:T(8,128)(2,1)} %get-tuple-element.36), calls=%async_computation.1 | async-start | bytes 3145728 | tf_op jit(solution)/shard_map/all_to_all | solution.py:546
  430.8 63.8 %copy-start = (bf16[32,3,16,512]{3,2,1,0:T(8,128)(2,1)}, bf16[32,3,16,512]{3,2,1,0:T(8,128)(2,1)S(1)}, u32[]{:S(2)}) copy-start(bf16[32,3,16,512]{3,2,1,0:T(8,128)(2,1)S(1)} %all-to-all-done.1.first_ref) | copy-start | bytes 4718596

commit v3 on v2

v3 whole, which is shorter than its diff:
```python
import functools
import math

import jax
import jax.numpy as jnp
from jax import lax
from jax.experimental import pallas as pl
from jax.experimental.pallas import tpu as pltpu
from jax.sharding import PartitionSpec as P

HEADS = 8
REACH = 2
KEY_TILE = 1024
QUERY_TILE = 128
ONES_ROWS = 16
QUARTERS = 4
FIRST = 2
LEAST_MASS = 1e-20
MOST_MASS = 1e30
VMEM_BYTES = 62 * 1024 * 1024
BF = jnp.bfloat16
F32 = jnp.float32


def ring_order(count):
    grids = {16: (4, 2, 2), 64: (4, 4, 4)}
    if count not in grids:
        return list(range(count))
    deep, tall, wide = grids[count]
    columns = [(0, x) for x in range(wide)]
    for y in range(1, tall):
        across = range(wide - 1, 0, -1) if y % 2 else range(1, wide)
        columns += [(y, x) for x in across]
    columns += [(y, 0) for y in range(tall - 1, 0, -1)]
    ring = []
    for at, (y, x) in enumerate(columns):
        along = range(deep) if at % 2 == 0 else range(deep - 1, -1, -1)
        ring += [(z * tall + y) * wide + x for z in along]
    return ring


def params(**more):
    return pltpu.CompilerParams(vmem_limit_bytes=VMEM_BYTES, **more)


def each(count, act):
    def step(i, carry):
        act(i)
        return carry

    lax.fori_loop(0, count, step, 0)


def send_kernel(
    order_ref, offsets_ref, places_ref, points_ref, gain_ref, out_ref, slot_ref, told_ref, points_s, normed_s, taken_s, in_sems, out_sems
):
    block_count, length, features = points_s.shape
    shards = places_ref.shape[0]
    capacity = out_ref.shape[0] // shards
    group = 4

    def copy_in(g):
        rows = pl.ds(g * group, group)
        return pltpu.make_async_copy(points_ref.at[rows], points_s.at[rows], in_sems.at[g])

    def copy_out(b):
        return pltpu.make_async_copy(normed_s.at[b], out_ref.at[slot_ref[b]], out_sems.at[b])

    each(block_count // group, lambda g: copy_in(g).start())

    def clear(d):
        taken_s[d] = 0
        for i in range(capacity):
            told_ref[d * capacity + i] = -1

    each(shards, clear)
    for i in range(offsets_ref.shape[0]):
        told_ref[shards * capacity + i] = offsets_ref[i]

    def place(b):
        position = order_ref[b]
        device = places_ref[lax.div(position, block_count)]
        rank = taken_s[device]
        taken_s[device] = rank + 1
        slot_ref[b] = device * capacity + rank
        told_ref[device * capacity + rank] = lax.rem(position, block_count)

    each(block_count, place)

    def normalise(g):
        copy_in(g).wait()
        values = points_s[pl.ds(g * group, group)].astype(F32).reshape(group * length, features)
        centred = values - jnp.mean(values, axis=-1, keepdims=True)
        spread = jnp.mean(jnp.square(centred), axis=-1, keepdims=True)
        result = (centred * lax.rsqrt(spread + 1e-05) * gain_ref[...]).astype(BF)
        normed_s[pl.ds(g * group, group)] = result.reshape(group, length, features)
        for i in range(group):
            copy_out(g * group + i).start()

    each(block_count // group, normalise)
    each(block_count, lambda b: copy_out(b).wait())


def normed_to_send(blocks, order, offsets, norm_gain, ring, capacity):
    block_count, length, features = blocks.shape
    shards = len(ring)
    return pl.pallas_call(
        send_kernel,
        grid_spec=pltpu.PrefetchScalarGridSpec(
            num_scalar_prefetch=3,
            grid=(1,),
            in_specs=[pl.BlockSpec(memory_space=pl.ANY), pl.BlockSpec((1, features), lambda p, *s: (0, 0))],
            out_specs=[pl.BlockSpec(memory_space=pl.ANY)] + [pl.BlockSpec(memory_space=pltpu.SMEM)] * 2,
            scratch_shapes=[
                pltpu.VMEM(blocks.shape, BF),
                pltpu.VMEM(blocks.shape, BF),
                pltpu.SMEM((shards,), jnp.int32),
                pltpu.SemaphoreType.DMA((block_count // 4,)),
                pltpu.SemaphoreType.DMA((block_count,)),
            ],
        ),
        out_shape=[
            jax.ShapeDtypeStruct((shards * capacity, length, features), BF),
            jax.ShapeDtypeStruct((block_count,), jnp.int32),
            jax.ShapeDtypeStruct((shards * capacity + offsets.shape[0],), jnp.int32),
        ],
        compiler_params=params(),
        name="send",
    )(order, offsets, jnp.asarray(ring, jnp.int32), blocks, norm_gain.reshape(1, features))


def sort_kernel(known_ref, ranges_ref, arrived_ref, *refs):
    *out_refs, picked_ref, set_ref, within_ref, held_s, in_sems, out_sems = refs
    patch_count, _, per_patch = held_s.shape[:3]
    half = patch_count // 2
    slot_count = arrived_ref.shape[0]
    entry = slot_count + patch_count
    capacity = slot_count // (known_ref.shape[0] // entry)
    my_place = lax.axis_index("seq")
    my_range = ranges_ref[my_place]

    def copy_in(patch, i):
        at = patch * per_patch + i
        return pltpu.make_async_copy(arrived_ref.at[picked_ref[at]], held_s.at[patch, :, i], in_sems.at[at])

    def copies_out(patch):
        for chunk, quarters in enumerate((slice(0, FIRST), slice(FIRST, QUARTERS))):
            count = quarters.stop - quarters.start
            out_ref = out_refs[2 * chunk + patch // half]
            yield pltpu.make_async_copy(
                held_s.at[patch, pl.ds(quarters.start, count)], out_ref.at[patch % half], out_sems.at[patch, chunk]
            )

    each(patch_count * per_patch, lambda i: picked_ref.__setitem__(i, 0))

    def find(sender):
        for rank in range(capacity):
            position = known_ref[sender * entry + my_place * capacity + rank]

            @pl.when(position >= 0)
            def _():
                picked_ref[position] = sender * capacity + rank

    each(slot_count // capacity, find)
    for patch in range(patch_count):
        for i in range(per_patch):
            copy_in(patch, i).start()
    for patch in range(patch_count):
        wanted = patch + known_ref[my_range * entry + slot_count + patch] + REACH
        set_ref[patch] = lax.div(wanted, half)
        within_ref[patch] = lax.rem(wanted, half)
    for patch in range(patch_count):
        for i in range(per_patch):
            copy_in(patch, i).wait()
        for copy in copies_out(patch):
            copy.start()
    for patch in range(patch_count):
        for copy in copies_out(patch):
            copy.wait()


def sorted_patches(arrived, known, ranges, block_count, patch_count):
    _, quarters, length, features = arrived.shape
    per_patch = block_count // patch_count
    half = patch_count // 2
    patch_shape = (quarters, per_patch, length, features)
    counts = (block_count, patch_count, patch_count)
    chunk_shapes = [(half, count, per_patch, length, features) for count in (FIRST, quarters - FIRST) for _ in range(2)]
    results = pl.pallas_call(
        sort_kernel,
        grid_spec=pltpu.PrefetchScalarGridSpec(
            num_scalar_prefetch=2,
            grid=(1,),
            in_specs=[pl.BlockSpec(memory_space=pl.ANY)],
            out_specs=[pl.BlockSpec(memory_space=pl.ANY)] * 4 + [pl.BlockSpec(memory_space=pltpu.SMEM)] * 3,
            scratch_shapes=[
                pltpu.VMEM((patch_count,) + patch_shape, BF),
                pltpu.SemaphoreType.DMA((block_count,)),
                pltpu.SemaphoreType.DMA((patch_count, 2)),
            ],
        ),
        out_shape=[jax.ShapeDtypeStruct(shape, BF) for shape in chunk_shapes]
        + [jax.ShapeDtypeStruct((count,), jnp.int32) for count in counts],
        compiler_params=params(),
        name="sort",
    )(known, jnp.asarray(ranges, jnp.int32), arrived)
    return [chunk.reshape(-1, features) for chunk in results[:4]], results[4:]


def home_kernel(slot_ref, points_ref, part_ref, *refs, start):
    out_ref, points_s, part_s, out_s, in_sems, out_sems = refs[-6:]
    block_count, quarters = points_s.shape[:2]
    group = block_count // out_sems.shape[0]

    def place(g):
        return pl.ds(g * group, group), pl.ds(start, quarters)

    def copies_in(g):
        sems = in_sems.at[g]
        yield pltpu.make_async_copy(points_ref.at[place(g)], points_s.at[pl.ds(g * group, group)], sems.at[0])
        for i in range(group):
            b = g * group + i
            yield pltpu.make_async_copy(part_ref.at[slot_ref[b]], part_s.at[b], sems.at[1 + i])

    def copy_out(g):
        return pltpu.make_async_copy(out_s.at[pl.ds(g * group, group)], out_ref.at[place(g)], out_sems.at[g])

    def begin(g):
        for copy in copies_in(g):
            copy.start()

    def add(g):
        for copy in copies_in(g):
            copy.wait()
        rows = pl.ds(g * group, group)
        out_s[rows] = (points_s[rows].astype(F32) + part_s[rows].astype(F32)).astype(BF)
        copy_out(g).start()

    each(block_count // group, begin)
    each(block_count // group, add)
    each(block_count // group, lambda g: copy_out(g).wait())


def home_sum(blocks, part, slots, start, result=None):
    block_count = blocks.shape[0]
    group = 4
    chunk_shape = (block_count,) + part.shape[1:]
    operands = (slots, blocks, part) + (() if result is None else (result,))
    return pl.pallas_call(
        functools.partial(home_kernel, start=start),
        grid_spec=pltpu.PrefetchScalarGridSpec(
            num_scalar_prefetch=1,
            grid=(1,),
            in_specs=[pl.BlockSpec(memory_space=pl.ANY)] * (len(operands) - 1),
            out_specs=pl.BlockSpec(memory_space=pl.ANY),
            scratch_shapes=[
                pltpu.VMEM(chunk_shape, BF),
                pltpu.VMEM(chunk_shape, BF),
                pltpu.VMEM(chunk_shape, BF),
                pltpu.SemaphoreType.DMA((block_count // group, 1 + group)),
                pltpu.SemaphoreType.DMA((block_count // group,)),
            ],
        ),
        out_shape=jax.ShapeDtypeStruct(blocks.shape, BF),
        input_output_aliases={} if result is None else {3: 0},
        compiler_params=params(),
        cost_estimate=cost(5),
        name="home",
    )(*operands)


def nt_dot(a, b):
    return lax.dot_general(a, b, (((1,), (1,)), ((), ())), preferred_element_type=F32)


def in_range(mass):
    good = jnp.logical_and(mass >= LEAST_MASS, mass <= MOST_MASS)
    return jnp.min(jnp.where(good, 1.0, 0.0)) > 0.5


def lone_head(pair, which, width):
    kept = pair[which * width : (which + 1) * width]
    blank = jnp.zeros_like(kept)
    return jnp.concatenate([kept, blank] if which == 0 else [blank, kept], axis=0)


def with_ones(values):
    return jnp.concatenate([values, jnp.ones((ONES_ROWS, values.shape[1]), BF)], axis=0)


def plain_head(query_ref, key_ref, value_ref, head, width):
    pair = 2 * width * (head // 2)
    query = lone_head(query_ref[pair : pair + 2 * width, :], head % 2, width)
    total = None
    for at in range(0, key_ref.shape[0], KEY_TILE):
        scores = jnp.dot(key_ref[at : at + KEY_TILE, pair : pair + 2 * width], query, preferred_element_type=F32)
        raised = jnp.exp(scores).astype(BF)
        values = with_ones(value_ref[head * width : (head + 1) * width, at : at + KEY_TILE])
        part = jnp.dot(values, raised, preferred_element_type=F32)
        total = part if total is None else total + part
    return total


def plain_sums(query_ref, pieces, before, width, emit):
    masses = []
    for head in range(query_ref.shape[0] // width):
        rows, one = slice(head * width, (head + 1) * width), slice(head, head + 1)
        sums = None
        for key_ref, value_ref in pieces:
            part = plain_head(query_ref, key_ref, value_ref, head, width)
            sums = part if sums is None else sums + part
        total, mass = sums[:width], sums[width : width + 1]
        if before is not None:
            total, mass = total + before[0][rows, :], mass + before[1][one, :]
        masses.append(mass)
        emit(rows, one, slice(None), total, mass, jnp.zeros_like(mass))
    good = in_range(jnp.concatenate(masses, axis=0))
    if before is not None:
        good = jnp.logical_and(good, jnp.max(jnp.abs(before[2][...])) == 0.0)
    return good


def shifted_sums(query_ref, pieces, before, width, emit):
    def step(tile):
        columns = pl.ds(pl.multiple_of(tile * QUERY_TILE, QUERY_TILE), QUERY_TILE)
        for head in range(query_ref.shape[0] // width):
            rows, one = slice(head * width, (head + 1) * width), slice(head, head + 1)
            pair = 2 * width * (head // 2)
            features = slice(pair, pair + 2 * width)
            query = lone_head(query_ref[features, columns], head % 2, width)
            total = mass = top = None
            if before is not None:
                total, mass, top = before[0][rows, columns], before[1][one, columns], before[2][one, columns]
            for key_ref, value_ref in pieces:
                scores = jnp.dot(key_ref[:, features], query, preferred_element_type=F32)
                highest = jnp.max(scores, axis=0, keepdims=True)
                if top is not None:
                    highest = jnp.maximum(highest, top)
                raised = jnp.exp(scores - highest).astype(BF)
                sums = jnp.dot(with_ones(value_ref[rows, :]), raised, preferred_element_type=F32)
                if top is None:
                    total, mass = sums[:width], sums[width : width + 1]
                else:
                    scale = jnp.exp(top - highest)
                    total, mass = total * scale + sums[:width], mass * scale + sums[width : width + 1]
                top = highest
            emit(rows, one, columns, total, mass, top)

    each(query_ref.shape[1] // QUERY_TILE, step)


def attend(query_ref, pieces, before, emit, finish=None):
    width = query_ref.shape[0] // HEADS
    good = plain_sums(query_ref, pieces, before, width, emit)
    if finish is not None:
        finish()

    @pl.when(jnp.logical_not(good))
    def _():
        shifted_sums(query_ref, pieces, before, width, emit)
        if finish is not None:
            finish()


def keep_in(total_ref, mass_ref, top_ref):
    def emit(rows, one, columns, total, mass, top):
        total_ref[rows, columns] = total
        mass_ref[one, columns] = mass
        top_ref[one, columns] = top

    return emit


def normalise_in(mixed_s):
    def emit(rows, one, columns, total, mass, top):
        mixed_s[rows, columns] = (total * (1.0 / mass)).astype(BF)

    return emit


def projected_out(picked_ref, wo_ref, out_ref, mixed_s):
    _, quarters, length, _ = out_ref.shape
    per_patch = mixed_s.shape[1] // (quarters * length)

    def finish():
        mixed = lax.dot_general(mixed_s[...], wo_ref[...], (((0,), (0,)), ((), ())), preferred_element_type=F32)
        mixed = mixed.astype(BF)
        for i in range(per_patch):
            slot = picked_ref[pl.program_id(0) * per_patch + i]
            for quarter in range(quarters):
                at = (quarter * per_patch + i) * length
                out_ref[slot, quarter] = mixed[at : at + length]

    return finish


def own_kernel(low0_ref, high0_ref, low1_ref, high1_ref, wk_ref, wqv_ref, *refs):
    query0_ref, query1_ref, key_ref, value_ref, *state_refs = refs
    patch = pl.program_id(0)
    half = pl.num_programs(0) // 2
    features = wk_ref.shape[0]

    def project(chunks):
        at = 0
        for normed_ref, query_ref in zip(chunks, (query0_ref, query1_ref)):
            normed = normed_ref[...]
            rows = slice(at, at + normed.shape[0])
            key_ref[rows, :] = jnp.dot(normed, wk_ref[...], preferred_element_type=F32).astype(BF)
            both = nt_dot(wqv_ref[...], normed)
            query_ref[...] = both[:features].astype(BF) * math.sqrt(HEADS / features)
            value_ref[:, rows] = both[features:].astype(BF)
            at = rows.stop

    @pl.when(patch < half)
    def _():
        project((low0_ref, low1_ref))

    @pl.when(patch >= half)
    def _():
        project((high0_ref, high1_ref))

    attend(query0_ref, [(key_ref, value_ref)], None, keep_in(*state_refs))


def along(p, *s):
    return (0, p)


def down(p, *s):
    return (p, 0)


def whole(p, *s):
    return (0, 0)


def cost(microseconds):
    return pl.CostEstimate(flops=microseconds * 10**9, bytes_accessed=28 * 10**6, transcendentals=0)


def split_specs(arrays, patch_count):
    return [pl.BlockSpec((part.shape[0], part.shape[1] // patch_count), along) for part in arrays]


def own_attention(chunks, wk, wqv, patch_count):
    features = wk.shape[0]
    half = patch_count // 2
    counts = [chunk.shape[0] // half for chunk in chunks]
    rows = counts[0] + counts[2]
    shapes = [
        jax.ShapeDtypeStruct((features, patch_count * counts[0]), BF),
        jax.ShapeDtypeStruct((features, patch_count * counts[2]), BF),
        jax.ShapeDtypeStruct((patch_count * rows, features), BF),
        jax.ShapeDtypeStruct((features, patch_count * rows), BF),
        jax.ShapeDtypeStruct((features, patch_count * counts[0]), F32),
        jax.ShapeDtypeStruct((HEADS, patch_count * counts[0]), F32),
        jax.ShapeDtypeStruct((HEADS, patch_count * counts[0]), F32),
    ]
    specs = split_specs(shapes, patch_count)
    specs[2] = pl.BlockSpec((rows, features), down)
    lower = lambda p: (jnp.minimum(p, half - 1), 0)
    upper = lambda p: (jnp.maximum(p - half, 0), 0)
    query0, query1, keys, values, *state = pl.pallas_call(
        own_kernel,
        grid=(patch_count,),
        in_specs=[
            pl.BlockSpec((count, features), upper if i % 2 else lower) for i, count in enumerate(counts)
        ]
        + [pl.BlockSpec(wk.shape, whole), pl.BlockSpec(wqv.shape, whole)],
        out_specs=specs,
        out_shape=shapes,
        compiler_params=params(),
        cost_estimate=cost(26),
        name="own",
    )(*chunks, wk, wqv)
    return query0, query1, keys, values, state


def partner_kernel(picked_ref, source_ref, within_ref, *refs, last):
    set_refs, refs = refs[:4], refs[4:]
    query_ref, *before = refs[:4]
    wk_ref, wv_ref = refs[4:6]
    if last:
        wo_ref, out_ref, key_ref, value_ref, normed_s, sems, mixed_s = refs[6:]
    else:
        key_ref, value_ref, *state_refs, normed_s, sems = refs[6:]
    patch = pl.program_id(0)
    rows = normed_s.shape[1]
    now = lax.rem(patch, 2)

    def copy(set_ref, which, at):
        return pltpu.make_async_copy(set_ref.at[pl.ds(which * rows, rows)], normed_s.at[at], sems.at[at])

    def begin(which):
        for number, set_ref in enumerate(set_refs):

            @pl.when(source_ref[which] == number)
            def _(set_ref=set_ref):
                copy(set_ref, within_ref[which], lax.rem(which, 2)).start()

    @pl.when(patch == 0)
    def _():
        begin(patch)

    @pl.when(patch + 1 < pl.num_programs(0))
    def _():
        begin(patch + 1)

    copy(set_refs[1], 0, now).wait()
    normed = normed_s[now]
    key_ref[...] = jnp.dot(normed, wk_ref[...], preferred_element_type=F32).astype(BF)
    value_ref[...] = nt_dot(wv_ref[...], normed).astype(BF)
    pieces = [(key_ref, value_ref)]
    if last:
        attend(query_ref, pieces, before, normalise_in(mixed_s), projected_out(picked_ref, wo_ref, out_ref, mixed_s))
    else:
        attend(query_ref, pieces, before, keep_in(*state_refs))


def partner_chunk(places, sets, query, state, wk, wqv, wo=None, out_shape=None):
    features = wk.shape[0]
    patch_count = places[1].shape[0]
    rows = sets[0].shape[0] // (patch_count // 2)
    last = wo is not None
    held = (query, *state)
    made = [
        jax.ShapeDtypeStruct((patch_count * rows, features), BF),
        jax.ShapeDtypeStruct((features, patch_count * rows), BF),
    ]
    made_specs = [pl.BlockSpec((rows, features), down), pl.BlockSpec((features, rows), along)]
    weights = (wk, wqv) + ((wo,) if last else ())
    weight_specs = [pl.BlockSpec(wk.shape, whole), pl.BlockSpec(wk.shape, lambda p, *s: (1, 0))]
    scratch = [pltpu.VMEM((2, rows, features), BF), pltpu.SemaphoreType.DMA((2,))]
    if last:
        weight_specs.append(pl.BlockSpec(wo.shape, whole))
        made = [jax.ShapeDtypeStruct(out_shape, BF)] + made
        made_specs = [pl.BlockSpec(out_shape, lambda p, *s: (0, 0, 0, 0))] + made_specs
        scratch.append(pltpu.VMEM((features, query.shape[1] // patch_count), BF))
    else:
        made += [jax.ShapeDtypeStruct(part.shape, part.dtype) for part in state]
        made_specs += split_specs(state, patch_count)
    return pl.pallas_call(
        functools.partial(partner_kernel, last=last),
        grid_spec=pltpu.PrefetchScalarGridSpec(
            num_scalar_prefetch=3,
            grid=(patch_count,),
            in_specs=[pl.BlockSpec(memory_space=pl.ANY)] * 4 + split_specs(held, patch_count) + weight_specs,
            out_specs=made_specs,
            scratch_shapes=scratch,
        ),
        out_shape=made,
        compiler_params=params(),
        cost_estimate=cost(15),
        name="partner_last" if last else "partner_next",
    )(*places, *sets, *held, *weights)


def rest_kernel(picked_ref, query_ref, *refs):
    *piece_refs, wo_ref, out_ref, mixed_s = refs
    pieces = list(zip(piece_refs[::2], piece_refs[1::2]))
    attend(query_ref, pieces, None, normalise_in(mixed_s), projected_out(picked_ref, wo_ref, out_ref, mixed_s))


def rest_attention(picked, query, pieces, wo, out_shape, patch_count):
    features = wo.shape[0]
    piece_specs = []
    for keys, _ in pieces:
        rows = keys.shape[0] // patch_count
        piece_specs += [pl.BlockSpec((rows, features), down), pl.BlockSpec((features, rows), along)]
    return pl.pallas_call(
        rest_kernel,
        grid_spec=pltpu.PrefetchScalarGridSpec(
            num_scalar_prefetch=1,
            grid=(patch_count,),
            in_specs=split_specs((query,), patch_count) + piece_specs + [pl.BlockSpec(wo.shape, whole)],
            out_specs=pl.BlockSpec(out_shape, lambda p, *s: (0, 0, 0, 0)),
            scratch_shapes=[pltpu.VMEM((features, query.shape[1] // patch_count), BF)],
        ),
        out_shape=jax.ShapeDtypeStruct(out_shape, BF),
        compiler_params=params(),
        cost_estimate=cost(38),
        name="rest",
    )(picked, query, *[array for piece in pieces for array in piece], wo)


def told_by_all(told):
    shards = lax.axis_size("seq")
    if shards & (shards - 1):
        return lax.all_gather(told, "seq", tiled=True)
    me = lax.axis_index("seq")
    step = 1
    while step < shards:
        other = lax.ppermute(told, "seq", [(place, place ^ step) for place in range(shards)])
        told = jnp.where((me & step) == 0, jnp.concatenate([told, other]), jnp.concatenate([other, told]))
        step *= 2
    return told


def exchanged(value):
    return lax.all_to_all(value, "seq", split_axis=0, concat_axis=0, tiled=True)


def body(points, order, offsets, norm_gain, w_qkv, w_out):
    features = points.shape[1]
    block_count = order.shape[0]
    block_rows = points.shape[0] // block_count
    patch_count = offsets.shape[0]
    shards = lax.axis_size("seq")
    capacity = (block_count + shards - 1) // shards
    ring = ring_order(shards)
    ring_next = [(ring[e], ring[(e + 1) % shards]) for e in range(shards)]
    ring_before = [(ring[e], ring[e - 1]) for e in range(shards)]
    ranges = [ring.index(place) for place in range(shards)]
    wk = w_qkv[:, features : 2 * features]
    wqv = jnp.concatenate([w_qkv[:, :features], w_qkv[:, 2 * features :]], axis=1).T

    blocks = points.reshape(block_count, block_rows, features)
    outgoing, slots, told = normed_to_send(blocks, order, offsets, norm_gain, ring, capacity)
    arrived = exchanged(outgoing).reshape(-1, QUARTERS, block_rows // QUARTERS, features)
    known = told_by_all(told)
    chunks, places = sorted_patches(arrived, known, ranges, block_count, patch_count)
    sets = []
    for low, high in (chunks[:2], chunks[2:]):
        left = lax.ppermute(high, "seq", ring_next)
        right = lax.ppermute(low, "seq", ring_before)
        sets.append((left, low, high, right))
    query0, query1, keys, values, state = own_attention(chunks, wk, wqv, patch_count)
    slot_count, _, length, _ = arrived.shape
    keys0, values0, *state = partner_chunk(places, sets[0], query0, state, wk, wqv)
    first, keys1, values1 = partner_chunk(
        places, sets[1], query0, state, wk, wqv, w_out, (slot_count, FIRST, length, features)
    )
    first_home = exchanged(first)
    pieces = [(keys, values), (keys0, values0), (keys1, values1)]
    rest = rest_attention(
        places[0], query1, pieces, w_out, (slot_count, QUARTERS - FIRST, length, features), patch_count
    )
    rest, first_home = lax.optimization_barrier((rest, first_home))
    rest_home = exchanged(rest)
    split_blocks = blocks.reshape(block_count, QUARTERS, block_rows // QUARTERS, features)
    result = home_sum(split_blocks, first_home, slots, 0)
    return home_sum(split_blocks, rest_home, slots, FIRST, result).reshape(-1, features)


def solution(mesh):
    return jax.shard_map(
        body,
        mesh=mesh,
        in_specs=(
            P(("scene", "seq"), None),
            P(("scene", "seq")),
            P(("scene", "seq")),
            P(),
            P(),
            P(),
        ),
        out_specs=P(("scene", "seq"), None),
        check_vma=False,
    )
```

time: 504 us -> 516 us (1.024)
  blocking collectives: 151 us -> 0 us
  waiting for transfers between devices: 1.41 us -> 127 us
  Pallas kernels: 324 us -> 353 us
  starting transfers between devices: 18 us -> 30.4 us
    unnamed x1 -> x0, blocking collectives: 87.6 us -> none
    ppermute x0 -> x4, waiting for transfers between devices: none -> 81.5 us  [told_by_all(): lax.ppermute(told, 'seq', [(place, place ^ step) for place in range(shard...]
    all_to_all x1 -> x0, blocking collectives: 63.8 us -> none  [exchanged(): return lax.all_to_all(value, 'seq', split_axis=0, concat_axis=0, tiled=True)]
    all_to_all x2 -> x3, waiting for transfers between devices: 1.41 us -> 45.7 us  [exchanged(): return lax.all_to_all(value, 'seq', split_axis=0, concat_axis=0, tiled=True)]
    pallas_call x4 -> x6, Pallas kernels: 312 us -> 341 us  [the longest x1 140 us: rest_attention(): pl.pallas_call(rest_kernel, grid_spec=pltpu.PrefetchScalarGridSpec(num_sc...]
    all_to_all x2 -> x3, starting transfers between devices: 13.2 us -> 20.1 us  [exchanged(): return lax.all_to_all(value, 'seq', split_axis=0, concat_axis=0, tiled=True)]
    ppermute x0 -> x4, starting transfers between devices: none -> 5.72 us  [told_by_all(): lax.ppermute(told, 'seq', [(place, place ^ step) for place in range(shard...]
  transfers between devices with their start and end apart: 4 -> 11, of which waited for: 1 -> 6; matrix products, arithmetic and copies ran while one was open for 1% -> 1% of each run, Pallas kernels for 47% -> 54%
where the time goes in v3:
time: 516 us; the launch traced here: 515 us
  Pallas kernels  353 us (68%)
  waiting for transfers between devices  127 us (25%)
  starting transfers between devices  30.4 us (6%)
    pallas_call x1, Pallas kernels, rest_attention(): pl.pallas_call(rest_kernel, grid_spec=pltpu.PrefetchScalarGridSpec(num_sc...  140 us
    pallas_call x2, Pallas kernels, partner_chunk(): pl.pallas_call(functools.partial(partner_kernel, last=last), grid_spec=pl...  114 us
    ppermute x4, waiting for transfers between devices, told_by_all(): lax.ppermute(told, 'seq', [(place, place ^ step) for place in range(shard...  81.5 us
    pallas_call x1, Pallas kernels, own_attention(): pl.pallas_call(own_kernel, grid=(patch_count,), in_specs=[pl.BlockSpec((c...  78.3 us
    all_to_all x3, waiting for transfers between devices, exchanged(): return lax.all_to_all(value, 'seq', split_axis=0, concat_axis=0, tiled=True)  45.7 us
    all_to_all x3, starting transfers between devices, exchanged(): return lax.all_to_all(value, 'seq', split_axis=0, concat_axis=0, tiled=True)  20.1 us
  transfers between devices with their start and end apart: 11, of which 6 were waited for; matrix products, arithmetic and copies ran while one was open for 1% of the time, Pallas kernels for 54%

profile of v3, /device:TPU:12, one launch (start us, length us, event | category | flops | bytes accessed | tf_op | source)
XLA Modules:
  0.0 515.3 jit_solution(7160750729414123851)
XLA Ops:
  0.0 6.6 %send.1 = (bf16[32,128,512]{2,1,0:T(8,128)(2,1)}, s32[32]{0:T(128)}, s32[36]{0:T(128)}) custom-call(s32[32]{0:T(128)} %order_ref.1, s32[4]{0:T(128)} %offsets_ref.1, s32[16]{0:T(128)} %constant.18.clone.places_ref, bf16[32,128,512]{2,1,0:T(8,128)(2,1)} %bitcast.11, f32[1,512]{1,0:T(1,128)} %bitcast.14), custom_call_target="tpu_custom_call" | custom-call | tf_op jit(solution)/shard_map/send/pallas_call | solution.py:107
  6.7 0.0 copy-start.1
  6.7 0.0 copy-start
  6.7 7.3 %all-to-all-start = ((bf16[32,128,512]{2,1,0:T(8,128)(2,1)}), bf16[32,128,512]{2,1,0:T(8,128)(2,1)}, u32[]{:S(2)}, u32[]{:S(2)}) async-start(bf16[32,128,512]{2,1,0:T(8,128)(2,1)} %get-tuple-element.34), calls=%async_computation | async-start | bytes 8388608 | tf_op jit(solution)/shard_map/all_to_all | solution.py:600
  14.0 0.0 copy-done.1
  14.0 1.5 collective-permute-start
  15.5 12.8 %collective-permute-done = s32[36]{0:T(128)S(1)} collective-permute-done((s32[36]{0:T(128)S(1)}, s32[36]{0:T(128)S(1)}, u32[]{:S(2)}, u32[]{:S(2)}) %collective-permute-start) | collective-permute-done | bytes 176 | tf_op jit(solution)/shard_map/ppermute | solution.py:593
  28.3 0.1 broadcast_select_fusion
  28.4 0.7 collective-permute-start.1
  29.1 2.9 collective-permute-done.1
  32.0 0.1 add_select_fusion.2
  32.1 1.4 collective-permute-start.2
  33.4 0.0 copy-done
  33.4 1.0 fusion
  34.5 0.2 copy.13
  34.7 0.2 copy.12
  34.9 49.7 %collective-permute-done.2 = s32[144]{0:T(256)S(1)} collective-permute-done((s32[144]{0:T(256)S(1)}, s32[144]{0:T(256)S(1)}, u32[]{:S(2)}, u32[]{:S(2)}) %collective-permute-start.2) | collective-permute-done | bytes 608 | tf_op jit(solution)/shard_map/ppermute | solution.py:593
  84.6 0.1 add_select_fusion.1
  84.7 2.1 collective-permute-start.3
  86.8 1.0 maximum_bitcast_fusion.wqv_ref.refs_9_
  87.8 16.1 %collective-permute-done.3 = s32[288]{0:T(512)S(1)} collective-permute-done((s32[288]{0:T(512)S(1)}, s32[288]{0:T(512)S(1)}, u32[]{:S(2)}, u32[]{:S(2)}) %collective-permute-start.3) | collective-permute-done | bytes 1184 | tf_op jit(solution)/shard_map/ppermute | solution.py:593
  104.0 0.7 add_select_fusion.known_ref
  104.6 3.6 all-to-all-done
  108.3 5.3 %sort.1 = (bf16[2,2,8,32,512]{4,3,2,1,0:T(8,128)(2,1)}, bf16[2,2,8,32,512]{4,3,2,1,0:T(8,128)(2,1)}, bf16[2,2,8,32,512]{4,3,2,1,0:T(8,128)(2,1)}, bf16[2,2,8,32,...) custom-call(s32[576]{0:T(1024)} %add_select_fusion.known_ref, s32[16]{0:T(128)} %constant.19.clone.ranges_ref, ...), custom_call_target="tpu_custom_call" | custom-call | tf_op jit(solution)/shard_map/sort/pallas_call | solution.py:189
  113.5 2.6 collective-permute-start.4
  116.1 0.0 collective-permute-start.5
  116.1 2.0 collective-permute-start.6
  118.1 0.0 collective-permute-start.7
  118.1 78.3 %own.1 = (bf16[512,2048]{1,0:T(8,128)(2,1)}, bf16[512,2048]{1,0:T(8,128)(2,1)}, bf16[4096,512]{1,0:T(8,128)(2,1)}, bf16[512,4096]{1,0:T(8,128)(2,1)}, f32[512,20...) custom-call(bf16[1024,512]{1,0:T(8,128)(2,1)} %bitcast.22, bf16[1024,512]{1,0:T(8,128)(2,1)} %bitcast.25, ...), custom_call_target="tpu_custom_call" | custom-call | flops 25999998976 | bytes 28000000 | tf_op jit(solution)/shard_map/own/pallas_call | solution.py:463
  196.4 0.0 collective-permute-done.4.refs_0_
  196.4 0.0 collective-permute-done.5.refs_3_
  196.4 55.3 %partner_next.1 = (bf16[2048,512]{1,0:T(8,128)(2,1)}, bf16[512,2048]{1,0:T(8,128)(2,1)}, f32[512,2048]{1,0:T(8,128)}, f32[8,2048]{1,0:T(8,128)}, f32[8,2048]{1,0:T(8,128)}) custom-call(s32[32]{0:T(128)} %get-tuple-element.35.picked_ref, s32[4]{0:T(128)} %get-tuple-element.43.source_ref, s32[4]{0:T(128)} %get-tuple-element.44.within_ref, ...), custom_call_target="tpu_custom_call" | custom-call | flops 15000000512 | bytes 28000000 | tf_op jit(solution)/shard_map/partner_next/pallas_call | solution.py:542
  251.7 0.0 collective-permute-done.6.refs_0_
  251.7 0.0 copy-start.2
  251.7 0.0 collective-permute-done.7.refs_3_
  251.7 1.0 copy-done.2
  252.7 58.8 %partner_last.1 = (bf16[32,2,32,512]{3,2,1,0:T(8,128)(2,1)}, bf16[2048,512]{1,0:T(8,128)(2,1)}, bf16[512,2048]{1,0:T(8,128)(2,1)}) custom-call(s32[32]{0:T(128)} %get-tuple-element.35.picked_ref, s32[4]{0:T(128)} %get-tuple-element.43.source_ref, s32[4]{0:T(128)} %get-tuple-element.44.within_ref, bf16[1024,512]{1,0:T(8,128)(2,1)} %copy-done.2, ...), custom_call_target="tpu_custom_call" | custom-call | flops 15000000512 | bytes 28000000 | tf_op jit(solution)/shard_map/partner_last/pallas_call | solution.py:542
  311.5 5.8 %all-to-all-start.1 = ((bf16[32,2,32,512]{3,2,1,0:T(8,128)(2,1)}), bf16[32,2,32,512]{3,2,1,0:T(8,128)(2,1)}, u32[]{:S(2)}, u32[]{:S(2)}) async-start(bf16[32,2,32,512]{3,2,1,0:T(8,128)(2,1)} %get-tuple-element.56), calls=%async_computation.1 | async-start | bytes 4194304 | tf_op jit(solution)/shard_map/all_to_all | solution.py:600
  317.4 140.2 %rest.1 = bf16[32,2,32,512]{3,2,1,0:T(8,128)(2,1)} custom-call(s32[32]{0:T(128)} %get-tuple-element.35.picked_ref, bf16[512,2048]{1,0:T(8,128)(2,1)} %get-tuple-element.40.query_ref, bf16[4096,512]{1,0:T(8,128)(2,1)} %get-tuple-element.41.refs_0_, bf16[512,4096]{1,0:T(8,128)(2,1)} %get-tuple-element.42.refs_1_, bf16[2048,512]{1,0:T(8,128)(2,1)} %get-tuple-element.49.refs_2_, ...), custom_call_target="tpu_custom_call" | custom-call | flops 38000001024 | bytes 28000000 | tf_op jit(solution)/shard_map/rest/pallas_call | solution.py:570
  457.6 0.0 all-to-all-done.1.part_ref
  457.6 6.9 %all-to-all-start.2 = ((bf16[32,2,32,512]{3,2,1,0:T(8,128)(2,1)}), bf16[32,2,32,512]{3,2,1,0:T(8,128)(2,1)}, u32[]{:S(2)}, u32[]{:S(2)}) async-start(bf16[32,2,32,512]{3,2,1,0:T(8,128)(2,1)} %rest.1), calls=%async_computation.2 | async-start | bytes 4194304 | tf_op jit(solution)/shard_map/all_to_all | solution.py:600
  464.5 4.3 home.2.refs_0_
  468.8 42.0 %all-to-all-done.2.part_ref = bf16[32,2,32,512]{3,2,1,0:T(8,128)(2,1)} async-done(((bf16[32,2,32,512]{3,2,1,0:T(8,128)(2,1)}), bf16[32,2,32,512]{3,2,1,0:T(8,128)(2,1)}, u32[]{:S(2)}, u32[]{:S(2)}) %all-to-all-start.2) | async-done | bytes 2097184 | tf_op jit(solution)/shard_map/all_to_all | solution.py:600
  510.8 4.3 home.3
Async XLA Ops:
  6.7 7.3 %copy-start.1 = (s32[36]{0:T(128)S(1)}, s32[36]{0:T(128)}, u32[]{:S(2)}) copy-start(s32[36]{0:T(128)} %get-tuple-element.33) | copy-start | bytes 436
  6.7 26.8 %copy-start = (bf16[512,1536]{1,0:T(8,128)(2,1)S(1)}, bf16[512,1536]{1,0:T(8,128)(2,1)}, u32[]{:S(2)}) copy-start(bf16[512,1536]{1,0:T(8,128)(2,1)} %param.12) | copy-start | bytes 4718596
  6.7 101.6 %all-to-all-start = ((bf16[32,128,512]{2,1,0:T(8,128)(2,1)}), bf16[32,128,512]{2,1,0:T(8,128)(2,1)}, u32[]{:S(2)}, u32[]{:S(2)}) async-start(bf16[32,128,512]{2,1,0:T(8,128)(2,1)} %get-tuple-element.34), calls=%async_computation | async-start | bytes 8388608 | tf_op jit(solution)/shard_map/all_to_all | solution.py:600
  14.0 14.3 %collective-permute-start = (s32[36]{0:T(128)S(1)}, s32[36]{0:T(128)S(1)}, u32[]{:S(2)}, u32[]{:S(2)}) collective-permute-start(s32[36]{0:T(128)S(1)} %copy-done.1), channel_id=1, source_target_pairs={{0,1},{1,0},{2,3},{3,2},{4,5},{5,4},{6,7},{7,6},{8,9},{9,8},{10,11... | collective-permute-start | bytes 440 | tf_op jit(solution)/shard_map/ppermute | solution.py:593
  28.4 3.6 collective-permute-start.1
  32.1 52.5 %collective-permute-start.2 = (s32[144]{0:T(256)S(1)}, s32[144]{0:T(256)S(1)}, u32[]{:S(2)}, u32[]{:S(2)}) collective-permute-start(s32[144]{0:T(256)S(1)} %add_select_fusion.2), channel_id=1, source_target_pairs={{0,4},{1,5},{2,6},{3,7},{4,0},{5,1},{6,2},{7,3},{8,12},{9,13},{10,... | collective-permute-start | bytes 1736 | tf_op jit(solution)/shard_map/ppermute | solution.py:593
  84.7 19.3 %collective-permute-start.3 = (s32[288]{0:T(512)S(1)}, s32[288]{0:T(512)S(1)}, u32[]{:S(2)}, u32[]{:S(2)}) collective-permute-start(s32[288]{0:T(512)S(1)} %add_select_fusion.1), channel_id=1, source_target_pairs={{0,8},{1,9},{2,10},{3,11},{4,12},{5,13},{6,14},{7,15},{8,0},{9,1},... | collective-permute-start | bytes 3464 | tf_op jit(solution)/shard_map/ppermute | solution.py:593
  113.5 82.9 %collective-permute-start.4 = (bf16[1024,512]{1,0:T(8,128)(2,1)}, bf16[1024,512]{1,0:T(8,128)(2,1)}, u32[]{:S(2)}, u32[]{:S(2)}) collective-permute-start(bf16[1024,512]{1,0:T(8,128)(2,1)} %bitcast.24), channel_id=1, source_target_pairs={{0,4},{4,8},{8,12},{12,13},{13,9},{9,5},{5,1},{1,3},{3,7},{7,11},{... | collective-permute-start | bytes 3145736 | tf_op jit(solution)/shard_map/ppermute | solution.py:624
  116.1 80.3 %collective-permute-start.5 = (bf16[1024,512]{1,0:T(8,128)(2,1)}, bf16[1024,512]{1,0:T(8,128)(2,1)}, u32[]{:S(2)}, u32[]{:S(2)}) collective-permute-start(bf16[1024,512]{1,0:T(8,128)(2,1)} %bitcast.21), channel_id=1, source_target_pairs={{0,2},{4,0},{8,4},{12,8},{13,12},{9,13},{5,9},{1,5},{3,1},{7,3},{1... | collective-permute-start | bytes 3145736 | tf_op jit(solution)/shard_map/ppermute | solution.py:625
  116.1 135.6 %collective-permute-start.6 = (bf16[1024,512]{1,0:T(8,128)(2,1)}, bf16[1024,512]{1,0:T(8,128)(2,1)S(1)}, u32[]{:S(2)}, u32[]{:S(2)}) collective-permute-start(bf16[1024,512]{1,0:T(8,128)(2,1)} %bitcast.18), channel_id=1, source_target_pairs={{0,4},{4,8},{8,12},{12,13},{13,9},{9,5},{5,1},{1,3},{3,7},{7,11},{... | collective-permute-start | bytes 3145736 | tf_op jit(solution)/shard_map/ppermute | solution.py:624
  118.1 133.6 %collective-permute-start.7 = (bf16[1024,512]{1,0:T(8,128)(2,1)}, bf16[1024,512]{1,0:T(8,128)(2,1)}, u32[]{:S(2)}, u32[]{:S(2)}) collective-permute-start(bf16[1024,512]{1,0:T(8,128)(2,1)} %bitcast.15), channel_id=1, source_target_pairs={{0,2},{4,0},{8,4},{12,8},{13,12},{9,13},{5,9},{1,5},{3,1},{7,3},{1... | collective-permute-start | bytes 3145736 | tf_op jit(solution)/shard_map/ppermute | solution.py:625
  251.7 1.0 copy-start.2
  311.5 146.0 %all-to-all-start.1 = ((bf16[32,2,32,512]{3,2,1,0:T(8,128)(2,1)}), bf16[32,2,32,512]{3,2,1,0:T(8,128)(2,1)}, u32[]{:S(2)}, u32[]{:S(2)}) async-start(bf16[32,2,32,512]{3,2,1,0:T(8,128)(2,1)} %get-tuple-element.56), calls=%async_computation.1 | async-start | bytes 4194304 | tf_op jit(solution)/shard_map/all_to_all | solution.py:600
  457.6 53.3 %all-to-all-start.2 = ((bf16[32,2,32,512]{3,2,1,0:T(8,128)(2,1)}), bf16[32,2,32,512]{3,2,1,0:T(8,128)(2,1)}, u32[]{:S(2)}, u32[]{:S(2)}) async-start(bf16[32,2,32,512]{3,2,1,0:T(8,128)(2,1)} %rest.1), calls=%async_computation.2 | async-start | bytes 4194304 | tf_op jit(solution)/shard_map/all_to_all | solution.py:600

commit v4 on v3

--- a/solution.py
+++ b/solution.py
@@ -10,11 +10,11 @@
 
 HEADS = 8
 REACH = 2
-KEY_TILE = 1024
+KEY_TILE = 512
 QUERY_TILE = 128
 ONES_ROWS = 16
-QUARTERS = 4
-FIRST = 2
+QUARTERS = 2
+FIRST = 1
 LEAST_MASS = 1e-20
 MOST_MASS = 1e30
 VMEM_BYTES = 62 * 1024 * 1024
@@ -288,32 +288,38 @@
     return jnp.concatenate([values, jnp.ones((ONES_ROWS, values.shape[1]), BF)], axis=0)
 
 
-def plain_head(query_ref, key_ref, value_ref, head, width):
-    pair = 2 * width * (head // 2)
-    query = lone_head(query_ref[pair : pair + 2 * width, :], head % 2, width)
-    total = None
+def plain_pair(query_ref, key_ref, value_ref, pair, width):
+    features = slice(2 * pair * width, 2 * (pair + 1) * width)
+    queries = query_ref[features, :]
+    count = queries.shape[1]
+    both = jnp.concatenate([lone_head(queries, which, width) for which in range(2)], axis=1)
+    sums = None
     for at in range(0, key_ref.shape[0], KEY_TILE):
-        scores = jnp.dot(key_ref[at : at + KEY_TILE, pair : pair + 2 * width], query, preferred_element_type=F32)
+        scores = jnp.dot(key_ref[at : at + KEY_TILE, features], both, preferred_element_type=F32)
         raised = jnp.exp(scores).astype(BF)
-        values = with_ones(value_ref[head * width : (head + 1) * width, at : at + KEY_TILE])
+        values = with_ones(value_ref[features, at : at + KEY_TILE])
         part = jnp.dot(values, raised, preferred_element_type=F32)
-        total = part if total is None else total + part
-    return total
+        sums = part if sums is None else sums + part
+    mass = slice(2 * width, 2 * width + 1)
+    return [
+        (sums[which * width : (which + 1) * width, columns], sums[mass, columns])
+        for which, columns in enumerate((slice(0, count), slice(count, 2 * count)))
+    ]
 
 
 def plain_sums(query_ref, pieces, before, width, emit):
     masses = []
-    for head in range(query_ref.shape[0] // width):
-        rows, one = slice(head * width, (head + 1) * width), slice(head, head + 1)
-        sums = None
-        for key_ref, value_ref in pieces:
-            part = plain_head(query_ref, key_ref, value_ref, head, width)
-            sums = part if sums is None else sums + part
-        total, mass = sums[:width], sums[width : width + 1]
-        if before is not None:
-            total, mass = total + before[0][rows, :], mass + before[1][one, :]
-        masses.append(mass)
-        emit(rows, one, slice(None), total, mass, jnp.zeros_like(mass))
+    for pair in range(query_ref.shape[0] // (2 * width)):
+        found = [plain_pair(query_ref, key_ref, value_ref, pair, width) for key_ref, value_ref in pieces]
+        for head in (2 * pair, 2 * pair + 1):
+            rows, one = slice(head * width, (head + 1) * width), slice(head, head + 1)
+            total, mass = found[0][head % 2]
+            for piece in found[1:]:
+                total, mass = total + piece[head % 2][0], mass + piece[head % 2][1]
+            if before is not None:
+                total, mass = total + before[0][rows, :], mass + before[1][one, :]
+            masses.append(mass)
+            emit(rows, one, slice(None), total, mass, jnp.zeros_like(mass))
     good = in_range(jnp.concatenate(masses, axis=0))
     if before is not None:
         good = jnp.logical_and(good, jnp.max(jnp.abs(before[2][...])) == 0.0)

time: 516 us -> 503 us (0.975)
  Pallas kernels: 353 us -> 340 us
    pallas_call x1, Pallas kernels: 140 us -> 134 us  [rest_attention(): pl.pallas_call(rest_kernel, grid_spec=pltpu.PrefetchScalarGridSpec(num_sc...]
    pallas_call x2, Pallas kernels: 114 us -> 108 us  [partner_chunk(): pl.pallas_call(functools.partial(partner_kernel, last=last), grid_spec=pl...]
  transfers between devices with their start and end apart: 11 -> 11, of which waited for: 6 -> 6; matrix products, arithmetic and copies ran while one was open for 1% -> 1% of each run, Pallas kernels for 54% -> 53%
where the time goes in v4:
time: 503 us
  Pallas kernels  340 us (68%)
  waiting for transfers between devices  127 us (25%)
  starting transfers between devices  30.4 us (6%)
    pallas_call x1, Pallas kernels, rest_attention(): pl.pallas_call(rest_kernel, grid_spec=pltpu.PrefetchScalarGridSpec(num_sc...  134 us
    pallas_call x2, Pallas kernels, partner_chunk(): pl.pallas_call(functools.partial(partner_kernel, last=last), grid_spec=pl...  108 us
    ppermute x4, waiting for transfers between devices, told_by_all(): lax.ppermute(told, 'seq', [(place, place ^ step) for place in range(shard...  81.5 us
    pallas_call x1, Pallas kernels, own_attention(): pl.pallas_call(own_kernel, grid=(patch_count,), in_specs=[pl.BlockSpec((c...  77.6 us
    all_to_all x3, waiting for transfers between devices, exchanged(): return lax.all_to_all(value, 'seq', split_axis=0, concat_axis=0, tiled=True)  45.7 us
    all_to_all x3, starting transfers between devices, exchanged(): return lax.all_to_all(value, 'seq', split_axis=0, concat_axis=0, tiled=True)  20.1 us
  transfers between devices with their start and end apart: 11, of which 6 were waited for; matrix products, arithmetic and copies ran while one was open for 1% of the time, Pallas kernels for 53%

profile of v4, /device:TPU:12, one launch (start us, length us, event | category | flops | bytes accessed | tf_op | source)
XLA Modules:
  0.0 502.6 jit_solution(2794013855158574534)
XLA Ops:
  0.0 6.6 %send.1 = (bf16[32,128,512]{2,1,0:T(8,128)(2,1)}, s32[32]{0:T(128)}, s32[36]{0:T(128)}) custom-call(s32[32]{0:T(128)} %order_ref.1, s32[4]{0:T(128)} %offsets_ref.1, s32[16]{0:T(128)} %constant.18.clone.places_ref, bf16[32,128,512]{2,1,0:T(8,128)(2,1)} %bitcast.11, f32[1,512]{1,0:T(1,128)} %bitcast.14), custom_call_target="tpu_custom_call" | custom-call | tf_op jit(solution)/shard_map/send/pallas_call | solution.py:107
  6.7 0.0 copy-start.1
  6.7 0.0 copy-start
  6.7 7.3 %all-to-all-start = ((bf16[32,128,512]{2,1,0:T(8,128)(2,1)}), bf16[32,128,512]{2,1,0:T(8,128)(2,1)}, u32[]{:S(2)}, u32[]{:S(2)}) async-start(bf16[32,128,512]{2,1,0:T(8,128)(2,1)} %get-tuple-element.34), calls=%async_computation | async-start | bytes 8388608 | tf_op jit(solution)/shard_map/all_to_all | solution.py:606
  14.0 0.0 copy-done.1
  14.0 1.5 collective-permute-start
  15.5 12.8 %collective-permute-done = s32[36]{0:T(128)S(1)} collective-permute-done((s32[36]{0:T(128)S(1)}, s32[36]{0:T(128)S(1)}, u32[]{:S(2)}, u32[]{:S(2)}) %collective-permute-start) | collective-permute-done | bytes 176 | tf_op jit(solution)/shard_map/ppermute | solution.py:599
  28.3 0.1 broadcast_select_fusion
  28.4 0.7 collective-permute-start.1
  29.1 2.9 collective-permute-done.1
  32.0 0.1 add_select_fusion.2
  32.1 1.4 collective-permute-start.2
  33.4 0.0 copy-done
  33.4 1.0 fusion
  34.5 0.2 copy.13
  34.7 0.2 copy.12
  34.9 49.7 %collective-permute-done.2 = s32[144]{0:T(256)S(1)} collective-permute-done((s32[144]{0:T(256)S(1)}, s32[144]{0:T(256)S(1)}, u32[]{:S(2)}, u32[]{:S(2)}) %collective-permute-start.2) | collective-permute-done | bytes 608 | tf_op jit(solution)/shard_map/ppermute | solution.py:599
  84.6 0.1 add_select_fusion.1
  84.7 2.1 collective-permute-start.3
  86.8 1.0 maximum_bitcast_fusion.wqv_ref.refs_9_
  87.8 16.1 %collective-permute-done.3 = s32[288]{0:T(512)S(1)} collective-permute-done((s32[288]{0:T(512)S(1)}, s32[288]{0:T(512)S(1)}, u32[]{:S(2)}, u32[]{:S(2)}) %collective-permute-start.3) | collective-permute-done | bytes 1184 | tf_op jit(solution)/shard_map/ppermute | solution.py:599
  104.0 0.7 add_select_fusion.known_ref
  104.6 3.6 all-to-all-done
  108.3 5.3 %sort.1 = (bf16[2,1,8,64,512]{4,3,2,1,0:T(8,128)(2,1)}, bf16[2,1,8,64,512]{4,3,2,1,0:T(8,128)(2,1)}, bf16[2,1,8,64,512]{4,3,2,1,0:T(8,128)(2,1)}, bf16[2,1,8,64,...) custom-call(s32[576]{0:T(1024)} %add_select_fusion.known_ref, s32[16]{0:T(128)} %constant.19.clone.ranges_ref, ...), custom_call_target="tpu_custom_call" | custom-call | tf_op jit(solution)/shard_map/sort/pallas_call | solution.py:189
  113.5 2.6 collective-permute-start.4
  116.1 0.0 collective-permute-start.5
  116.1 2.0 collective-permute-start.6
  118.1 0.0 collective-permute-start.7
  118.1 77.6 %own.1 = (bf16[512,2048]{1,0:T(8,128)(2,1)}, bf16[512,2048]{1,0:T(8,128)(2,1)}, bf16[4096,512]{1,0:T(8,128)(2,1)}, bf16[512,4096]{1,0:T(8,128)(2,1)}, f32[512,20...) custom-call(bf16[1024,512]{1,0:T(8,128)(2,1)} %bitcast.22, bf16[1024,512]{1,0:T(8,128)(2,1)} %bitcast.25, ...), custom_call_target="tpu_custom_call" | custom-call | flops 25999998976 | bytes 28000000 | tf_op jit(solution)/shard_map/own/pallas_call | solution.py:469
  195.8 0.0 collective-permute-done.4.refs_0_
  195.8 0.0 collective-permute-done.5.refs_3_
  195.8 52.4 %partner_next.1 = (bf16[2048,512]{1,0:T(8,128)(2,1)}, bf16[512,2048]{1,0:T(8,128)(2,1)}, f32[512,2048]{1,0:T(8,128)}, f32[8,2048]{1,0:T(8,128)}, f32[8,2048]{1,0:T(8,128)}) custom-call(s32[32]{0:T(128)} %get-tuple-element.35.picked_ref, s32[4]{0:T(128)} %get-tuple-element.43.source_ref, s32[4]{0:T(128)} %get-tuple-element.44.within_ref, ...), custom_call_target="tpu_custom_call" | custom-call | flops 15000000512 | bytes 28000000 | tf_op jit(solution)/shard_map/partner_next/pallas_call | solution.py:548
  248.2 0.0 collective-permute-done.6.refs_0_
  248.2 0.0 copy-start.2
  248.2 0.0 collective-permute-done.7.refs_3_
  248.2 1.0 copy-done.2
  249.2 56.0 %partner_last.1 = (bf16[32,1,64,512]{3,2,1,0:T(8,128)(2,1)}, bf16[2048,512]{1,0:T(8,128)(2,1)}, bf16[512,2048]{1,0:T(8,128)(2,1)}) custom-call(s32[32]{0:T(128)} %get-tuple-element.35.picked_ref, s32[4]{0:T(128)} %get-tuple-element.43.source_ref, s32[4]{0:T(128)} %get-tuple-element.44.within_ref, bf16[1024,512]{1,0:T(8,128)(2,1)} %copy-done.2, ...), custom_call_target="tpu_custom_call" | custom-call | flops 15000000512 | bytes 28000000 | tf_op jit(solution)/shard_map/partner_last/pallas_call | solution.py:548
  305.2 5.8 %all-to-all-start.1 = ((bf16[32,1,64,512]{3,2,1,0:T(8,128)(2,1)}), bf16[32,1,64,512]{3,2,1,0:T(8,128)(2,1)}, u32[]{:S(2)}, u32[]{:S(2)}) async-start(bf16[32,1,64,512]{3,2,1,0:T(8,128)(2,1)} %get-tuple-element.56), calls=%async_computation.1 | async-start | bytes 4194304 | tf_op jit(solution)/shard_map/all_to_all | solution.py:606
  311.1 133.8 %rest.1 = bf16[32,1,64,512]{3,2,1,0:T(8,128)(2,1)} custom-call(s32[32]{0:T(128)} %get-tuple-element.35.picked_ref, bf16[512,2048]{1,0:T(8,128)(2,1)} %get-tuple-element.40.query_ref, bf16[4096,512]{1,0:T(8,128)(2,1)} %get-tuple-element.41.refs_0_, bf16[512,4096]{1,0:T(8,128)(2,1)} %get-tuple-element.42.refs_1_, bf16[2048,512]{1,0:T(8,128)(2,1)} %get-tuple-element.49.refs_2_, ...), custom_call_target="tpu_custom_call" | custom-call | flops 38000001024 | bytes 28000000 | tf_op jit(solution)/shard_map/rest/pallas_call | solution.py:576
  444.9 0.0 all-to-all-done.1.part_ref
  444.9 6.9 %all-to-all-start.2 = ((bf16[32,1,64,512]{3,2,1,0:T(8,128)(2,1)}), bf16[32,1,64,512]{3,2,1,0:T(8,128)(2,1)}, u32[]{:S(2)}, u32[]{:S(2)}) async-start(bf16[32,1,64,512]{3,2,1,0:T(8,128)(2,1)} %rest.1), calls=%async_computation.2 | async-start | bytes 4194304 | tf_op jit(solution)/shard_map/all_to_all | solution.py:606
  451.8 4.3 home.2.refs_0_
  456.1 42.0 %all-to-all-done.2.part_ref = bf16[32,1,64,512]{3,2,1,0:T(8,128)(2,1)} async-done(((bf16[32,1,64,512]{3,2,1,0:T(8,128)(2,1)}), bf16[32,1,64,512]{3,2,1,0:T(8,128)(2,1)}, u32[]{:S(2)}, u32[]{:S(2)}) %all-to-all-start.2) | async-done | bytes 2097184 | tf_op jit(solution)/shard_map/all_to_all | solution.py:606
  498.1 4.3 home.3
Async XLA Ops:
  6.7 7.3 %copy-start.1 = (s32[36]{0:T(128)S(1)}, s32[36]{0:T(128)}, u32[]{:S(2)}) copy-start(s32[36]{0:T(128)} %get-tuple-element.33) | copy-start | bytes 436
  6.7 26.8 %copy-start = (bf16[512,1536]{1,0:T(8,128)(2,1)S(1)}, bf16[512,1536]{1,0:T(8,128)(2,1)}, u32[]{:S(2)}) copy-start(bf16[512,1536]{1,0:T(8,128)(2,1)} %param.12) | copy-start | bytes 4718596
  6.7 101.6 %all-to-all-start = ((bf16[32,128,512]{2,1,0:T(8,128)(2,1)}), bf16[32,128,512]{2,1,0:T(8,128)(2,1)}, u32[]{:S(2)}, u32[]{:S(2)}) async-start(bf16[32,128,512]{2,1,0:T(8,128)(2,1)} %get-tuple-element.34), calls=%async_computation | async-start | bytes 8388608 | tf_op jit(solution)/shard_map/all_to_all | solution.py:606
  14.0 14.3 %collective-permute-start = (s32[36]{0:T(128)S(1)}, s32[36]{0:T(128)S(1)}, u32[]{:S(2)}, u32[]{:S(2)}) collective-permute-start(s32[36]{0:T(128)S(1)} %copy-done.1), channel_id=1, source_target_pairs={{0,1},{1,0},{2,3},{3,2},{4,5},{5,4},{6,7},{7,6},{8,9},{9,8},{10,11... | collective-permute-start | bytes 440 | tf_op jit(solution)/shard_map/ppermute | solution.py:599
  28.4 3.6 collective-permute-start.1
  32.1 52.5 %collective-permute-start.2 = (s32[144]{0:T(256)S(1)}, s32[144]{0:T(256)S(1)}, u32[]{:S(2)}, u32[]{:S(2)}) collective-permute-start(s32[144]{0:T(256)S(1)} %add_select_fusion.2), channel_id=1, source_target_pairs={{0,4},{1,5},{2,6},{3,7},{4,0},{5,1},{6,2},{7,3},{8,12},{9,13},{10,... | collective-permute-start | bytes 1736 | tf_op jit(solution)/shard_map/ppermute | solution.py:599
  84.7 19.3 %collective-permute-start.3 = (s32[288]{0:T(512)S(1)}, s32[288]{0:T(512)S(1)}, u32[]{:S(2)}, u32[]{:S(2)}) collective-permute-start(s32[288]{0:T(512)S(1)} %add_select_fusion.1), channel_id=1, source_target_pairs={{0,8},{1,9},{2,10},{3,11},{4,12},{5,13},{6,14},{7,15},{8,0},{9,1},... | collective-permute-start | bytes 3464 | tf_op jit(solution)/shard_map/ppermute | solution.py:599
  113.5 82.2 %collective-permute-start.4 = (bf16[1024,512]{1,0:T(8,128)(2,1)}, bf16[1024,512]{1,0:T(8,128)(2,1)}, u32[]{:S(2)}, u32[]{:S(2)}) collective-permute-start(bf16[1024,512]{1,0:T(8,128)(2,1)} %bitcast.24), channel_id=1, source_target_pairs={{0,4},{4,8},{8,12},{12,13},{13,9},{9,5},{5,1},{1,3},{3,7},{7,11},{... | collective-permute-start | bytes 3145736 | tf_op jit(solution)/shard_map/ppermute | solution.py:630
  116.1 79.7 %collective-permute-start.5 = (bf16[1024,512]{1,0:T(8,128)(2,1)}, bf16[1024,512]{1,0:T(8,128)(2,1)}, u32[]{:S(2)}, u32[]{:S(2)}) collective-permute-start(bf16[1024,512]{1,0:T(8,128)(2,1)} %bitcast.21), channel_id=1, source_target_pairs={{0,2},{4,0},{8,4},{12,8},{13,12},{9,13},{5,9},{1,5},{3,1},{7,3},{1... | collective-permute-start | bytes 3145736 | tf_op jit(solution)/shard_map/ppermute | solution.py:631
  116.1 132.1 %collective-permute-start.6 = (bf16[1024,512]{1,0:T(8,128)(2,1)}, bf16[1024,512]{1,0:T(8,128)(2,1)S(1)}, u32[]{:S(2)}, u32[]{:S(2)}) collective-permute-start(bf16[1024,512]{1,0:T(8,128)(2,1)} %bitcast.18), channel_id=1, source_target_pairs={{0,4},{4,8},{8,12},{12,13},{13,9},{9,5},{5,1},{1,3},{3,7},{7,11},{... | collective-permute-start | bytes 3145736 | tf_op jit(solution)/shard_map/ppermute | solution.py:630
  118.1 130.1 %collective-permute-start.7 = (bf16[1024,512]{1,0:T(8,128)(2,1)}, bf16[1024,512]{1,0:T(8,128)(2,1)}, u32[]{:S(2)}, u32[]{:S(2)}) collective-permute-start(bf16[1024,512]{1,0:T(8,128)(2,1)} %bitcast.15), channel_id=1, source_target_pairs={{0,2},{4,0},{8,4},{12,8},{13,12},{9,13},{5,9},{1,5},{3,1},{7,3},{1... | collective-permute-start | bytes 3145736 | tf_op jit(solution)/shard_map/ppermute | solution.py:631
  248.2 1.0 copy-start.2
  305.2 139.7 %all-to-all-start.1 = ((bf16[32,1,64,512]{3,2,1,0:T(8,128)(2,1)}), bf16[32,1,64,512]{3,2,1,0:T(8,128)(2,1)}, u32[]{:S(2)}, u32[]{:S(2)}) async-start(bf16[32,1,64,512]{3,2,1,0:T(8,128)(2,1)} %get-tuple-element.56), calls=%async_computation.1 | async-start | bytes 4194304 | tf_op jit(solution)/shard_map/all_to_all | solution.py:606
  444.9 53.3 %all-to-all-start.2 = ((bf16[32,1,64,512]{3,2,1,0:T(8,128)(2,1)}), bf16[32,1,64,512]{3,2,1,0:T(8,128)(2,1)}, u32[]{:S(2)}, u32[]{:S(2)}) async-start(bf16[32,1,64,512]{3,2,1,0:T(8,128)(2,1)} %rest.1), calls=%async_computation.2 | async-start | bytes 4194304 | tf_op jit(solution)/shard_map/all_to_all | solution.py:606

commit v5 on v4

--- a/solution.py
+++ b/solution.py
@@ -139,9 +139,9 @@
     my_place = lax.axis_index("seq")
     my_range = ranges_ref[my_place]
 
-    def copy_in(patch, i):
-        at = patch * per_patch + i
-        return pltpu.make_async_copy(arrived_ref.at[picked_ref[at]], held_s.at[patch, :, i], in_sems.at[at])
+    def copy_in(position, slot):
+        place = held_s.at[lax.div(position, per_patch), :, lax.rem(position, per_patch)]
+        return pltpu.make_async_copy(arrived_ref.at[slot], place, in_sems.at[position])
 
     def copies_out(patch):
         for chunk, quarters in enumerate((slice(0, FIRST), slice(FIRST, QUARTERS))):
@@ -151,27 +151,24 @@
                 held_s.at[patch, pl.ds(quarters.start, count)], out_ref.at[patch % half], out_sems.at[patch, chunk]
             )
 
-    each(patch_count * per_patch, lambda i: picked_ref.__setitem__(i, 0))
-
     def find(sender):
         for rank in range(capacity):
+            slot = sender * capacity + rank
             position = known_ref[sender * entry + my_place * capacity + rank]
 
             @pl.when(position >= 0)
             def _():
-                picked_ref[position] = sender * capacity + rank
+                copy_in(position, slot).start()
+                picked_ref[position] = slot
 
     each(slot_count // capacity, find)
-    for patch in range(patch_count):
-        for i in range(per_patch):
-            copy_in(patch, i).start()
     for patch in range(patch_count):
         wanted = patch + known_ref[my_range * entry + slot_count + patch] + REACH
         set_ref[patch] = lax.div(wanted, half)
         within_ref[patch] = lax.rem(wanted, half)
     for patch in range(patch_count):
         for i in range(per_patch):
-            copy_in(patch, i).wait()
+            copy_in(patch * per_patch + i, 0).wait()
         for copy in copies_out(patch):
             copy.start()
     for patch in range(patch_count):

time: 503 us -> 504 us (level)
  no operation moved by 1% of the time
where the time goes in v5:
time: 504 us; the launch traced here: 503 us
  Pallas kernels  341 us (68%)
  waiting for transfers between devices  127 us (25%)
  starting transfers between devices  30.5 us (6%)
    pallas_call x1, Pallas kernels, rest_attention(): pl.pallas_call(rest_kernel, grid_spec=pltpu.PrefetchScalarGridSpec(num_sc...  134 us
    pallas_call x2, Pallas kernels, partner_chunk(): pl.pallas_call(functools.partial(partner_kernel, last=last), grid_spec=pl...  108 us
    ppermute x4, waiting for transfers between devices, told_by_all(): lax.ppermute(told, 'seq', [(place, place ^ step) for place in range(shard...  81.5 us
    pallas_call x1, Pallas kernels, own_attention(): pl.pallas_call(own_kernel, grid=(patch_count,), in_specs=[pl.BlockSpec((c...  77.6 us
    all_to_all x3, waiting for transfers between devices, exchanged(): return lax.all_to_all(value, 'seq', split_axis=0, concat_axis=0, tiled=True)  45.4 us
    all_to_all x3, starting transfers between devices, exchanged(): return lax.all_to_all(value, 'seq', split_axis=0, concat_axis=0, tiled=True)  20 us
  transfers between devices with their start and end apart: 11, of which 6 were waited for; matrix products, arithmetic and copies ran while one was open for 1% of the time, Pallas kernels for 53%

profile of v5, /device:TPU:12, one launch (start us, length us, event | category | flops | bytes accessed | tf_op | source)
XLA Modules:
  0.0 503.1 jit_solution(10269807597276918794)
XLA Ops:
  0.0 6.6 %send.1 = (bf16[32,128,512]{2,1,0:T(8,128)(2,1)}, s32[32]{0:T(128)}, s32[36]{0:T(128)}) custom-call(s32[32]{0:T(128)} %order_ref.1, s32[4]{0:T(128)} %offsets_ref.1, s32[16]{0:T(128)} %constant.18.clone.places_ref, bf16[32,128,512]{2,1,0:T(8,128)(2,1)} %bitcast.11, f32[1,512]{1,0:T(1,128)} %bitcast.14), custom_call_target="tpu_custom_call" | custom-call | tf_op jit(solution)/shard_map/send/pallas_call | solution.py:107
  6.7 0.0 copy-start.1
  6.7 0.0 copy-start
  6.7 7.3 %all-to-all-start = ((bf16[32,128,512]{2,1,0:T(8,128)(2,1)}), bf16[32,128,512]{2,1,0:T(8,128)(2,1)}, u32[]{:S(2)}, u32[]{:S(2)}) async-start(bf16[32,128,512]{2,1,0:T(8,128)(2,1)} %get-tuple-element.34), calls=%async_computation | async-start | bytes 8388608 | tf_op jit(solution)/shard_map/all_to_all | solution.py:603
  14.0 0.0 copy-done.1
  14.0 1.5 collective-permute-start
  15.5 12.8 %collective-permute-done = s32[36]{0:T(128)S(1)} collective-permute-done((s32[36]{0:T(128)S(1)}, s32[36]{0:T(128)S(1)}, u32[]{:S(2)}, u32[]{:S(2)}) %collective-permute-start) | collective-permute-done | bytes 176 | tf_op jit(solution)/shard_map/ppermute | solution.py:596
  28.3 0.1 broadcast_select_fusion
  28.4 0.7 collective-permute-start.1
  29.1 2.9 collective-permute-done.1
  32.0 0.1 add_select_fusion.2
  32.1 1.4 collective-permute-start.2
  33.4 0.0 copy-done
  33.4 1.0 fusion
  34.5 0.2 copy.13
  34.7 0.2 copy.12
  34.9 49.7 %collective-permute-done.2 = s32[144]{0:T(256)S(1)} collective-permute-done((s32[144]{0:T(256)S(1)}, s32[144]{0:T(256)S(1)}, u32[]{:S(2)}, u32[]{:S(2)}) %collective-permute-start.2) | collective-permute-done | bytes 608 | tf_op jit(solution)/shard_map/ppermute | solution.py:596
  84.6 0.1 add_select_fusion.1
  84.7 2.1 collective-permute-start.3
  86.8 1.0 maximum_bitcast_fusion.wqv_ref.refs_9_
  87.8 16.1 %collective-permute-done.3 = s32[288]{0:T(512)S(1)} collective-permute-done((s32[288]{0:T(512)S(1)}, s32[288]{0:T(512)S(1)}, u32[]{:S(2)}, u32[]{:S(2)}) %collective-permute-start.3) | collective-permute-done | bytes 1184 | tf_op jit(solution)/shard_map/ppermute | solution.py:596
  104.0 0.7 add_select_fusion.known_ref
  104.6 3.6 all-to-all-done
  108.3 5.8 %sort.1 = (bf16[2,1,8,64,512]{4,3,2,1,0:T(8,128)(2,1)}, bf16[2,1,8,64,512]{4,3,2,1,0:T(8,128)(2,1)}, bf16[2,1,8,64,512]{4,3,2,1,0:T(8,128)(2,1)}, bf16[2,1,8,64,...) custom-call(s32[576]{0:T(1024)} %add_select_fusion.known_ref, s32[16]{0:T(128)} %constant.19.clone.ranges_ref, ...), custom_call_target="tpu_custom_call" | custom-call | tf_op jit(solution)/shard_map/sort/pallas_call | solution.py:186
  114.0 2.7 collective-permute-start.4
  116.8 0.0 collective-permute-start.5
  116.8 2.0 collective-permute-start.6
  118.8 0.0 collective-permute-start.7
  118.8 77.6 %own.1 = (bf16[512,2048]{1,0:T(8,128)(2,1)}, bf16[512,2048]{1,0:T(8,128)(2,1)}, bf16[4096,512]{1,0:T(8,128)(2,1)}, bf16[512,4096]{1,0:T(8,128)(2,1)}, f32[512,20...) custom-call(bf16[1024,512]{1,0:T(8,128)(2,1)} %bitcast.22, bf16[1024,512]{1,0:T(8,128)(2,1)} %bitcast.25, ...), custom_call_target="tpu_custom_call" | custom-call | flops 25999998976 | bytes 28000000 | tf_op jit(solution)/shard_map/own/pallas_call | solution.py:466
  196.5 0.0 collective-permute-done.4.refs_0_
  196.5 0.0 collective-permute-done.5.refs_3_
  196.5 52.4 %partner_next.1 = (bf16[2048,512]{1,0:T(8,128)(2,1)}, bf16[512,2048]{1,0:T(8,128)(2,1)}, f32[512,2048]{1,0:T(8,128)}, f32[8,2048]{1,0:T(8,128)}, f32[8,2048]{1,0:T(8,128)}) custom-call(s32[32]{0:T(128)} %get-tuple-element.35.picked_ref, s32[4]{0:T(128)} %get-tuple-element.43.source_ref, s32[4]{0:T(128)} %get-tuple-element.44.within_ref, ...), custom_call_target="tpu_custom_call" | custom-call | flops 15000000512 | bytes 28000000 | tf_op jit(solution)/shard_map/partner_next/pallas_call | solution.py:545
  248.9 0.0 collective-permute-done.6.refs_0_
  248.9 0.0 copy-start.2
  248.9 0.0 collective-permute-done.7.refs_3_
  248.9 1.0 copy-done.2
  249.9 56.0 %partner_last.1 = (bf16[32,1,64,512]{3,2,1,0:T(8,128)(2,1)}, bf16[2048,512]{1,0:T(8,128)(2,1)}, bf16[512,2048]{1,0:T(8,128)(2,1)}) custom-call(s32[32]{0:T(128)} %get-tuple-element.35.picked_ref, s32[4]{0:T(128)} %get-tuple-element.43.source_ref, s32[4]{0:T(128)} %get-tuple-element.44.within_ref, bf16[1024,512]{1,0:T(8,128)(2,1)} %copy-done.2, ...), custom_call_target="tpu_custom_call" | custom-call | flops 15000000512 | bytes 28000000 | tf_op jit(solution)/shard_map/partner_last/pallas_call | solution.py:545
  305.9 5.7 %all-to-all-start.1 = ((bf16[32,1,64,512]{3,2,1,0:T(8,128)(2,1)}), bf16[32,1,64,512]{3,2,1,0:T(8,128)(2,1)}, u32[]{:S(2)}, u32[]{:S(2)}) async-start(bf16[32,1,64,512]{3,2,1,0:T(8,128)(2,1)} %get-tuple-element.56), calls=%async_computation.1 | async-start | bytes 4194304 | tf_op jit(solution)/shard_map/all_to_all | solution.py:603
  311.7 133.8 %rest.1 = bf16[32,1,64,512]{3,2,1,0:T(8,128)(2,1)} custom-call(s32[32]{0:T(128)} %get-tuple-element.35.picked_ref, bf16[512,2048]{1,0:T(8,128)(2,1)} %get-tuple-element.40.query_ref, bf16[4096,512]{1,0:T(8,128)(2,1)} %get-tuple-element.41.refs_0_, bf16[512,4096]{1,0:T(8,128)(2,1)} %get-tuple-element.42.refs_1_, bf16[2048,512]{1,0:T(8,128)(2,1)} %get-tuple-element.49.refs_2_, ...), custom_call_target="tpu_custom_call" | custom-call | flops 38000001024 | bytes 28000000 | tf_op jit(solution)/shard_map/rest/pallas_call | solution.py:573
  445.5 0.0 all-to-all-done.1.part_ref
  445.5 7.0 %all-to-all-start.2 = ((bf16[32,1,64,512]{3,2,1,0:T(8,128)(2,1)}), bf16[32,1,64,512]{3,2,1,0:T(8,128)(2,1)}, u32[]{:S(2)}, u32[]{:S(2)}) async-start(bf16[32,1,64,512]{3,2,1,0:T(8,128)(2,1)} %rest.1), calls=%async_computation.2 | async-start | bytes 4194304 | tf_op jit(solution)/shard_map/all_to_all | solution.py:603
  452.5 4.3 home.2.refs_0_
  456.8 41.8 %all-to-all-done.2.part_ref = bf16[32,1,64,512]{3,2,1,0:T(8,128)(2,1)} async-done(((bf16[32,1,64,512]{3,2,1,0:T(8,128)(2,1)}), bf16[32,1,64,512]{3,2,1,0:T(8,128)(2,1)}, u32[]{:S(2)}, u32[]{:S(2)}) %all-to-all-start.2) | async-done | bytes 2097184 | tf_op jit(solution)/shard_map/all_to_all | solution.py:603
  498.6 4.3 home.3
Async XLA Ops:
  6.7 7.3 %copy-start.1 = (s32[36]{0:T(128)S(1)}, s32[36]{0:T(128)}, u32[]{:S(2)}) copy-start(s32[36]{0:T(128)} %get-tuple-element.33) | copy-start | bytes 436
  6.7 26.8 %copy-start = (bf16[512,1536]{1,0:T(8,128)(2,1)S(1)}, bf16[512,1536]{1,0:T(8,128)(2,1)}, u32[]{:S(2)}) copy-start(bf16[512,1536]{1,0:T(8,128)(2,1)} %param.12) | copy-start | bytes 4718596
  6.7 101.6 %all-to-all-start = ((bf16[32,128,512]{2,1,0:T(8,128)(2,1)}), bf16[32,128,512]{2,1,0:T(8,128)(2,1)}, u32[]{:S(2)}, u32[]{:S(2)}) async-start(bf16[32,128,512]{2,1,0:T(8,128)(2,1)} %get-tuple-element.34), calls=%async_computation | async-start | bytes 8388608 | tf_op jit(solution)/shard_map/all_to_all | solution.py:603
  14.0 14.3 %collective-permute-start = (s32[36]{0:T(128)S(1)}, s32[36]{0:T(128)S(1)}, u32[]{:S(2)}, u32[]{:S(2)}) collective-permute-start(s32[36]{0:T(128)S(1)} %copy-done.1), channel_id=1, source_target_pairs={{0,1},{1,0},{2,3},{3,2},{4,5},{5,4},{6,7},{7,6},{8,9},{9,8},{10,11... | collective-permute-start | bytes 440 | tf_op jit(solution)/shard_map/ppermute | solution.py:596
  28.4 3.6 collective-permute-start.1
  32.1 52.5 %collective-permute-start.2 = (s32[144]{0:T(256)S(1)}, s32[144]{0:T(256)S(1)}, u32[]{:S(2)}, u32[]{:S(2)}) collective-permute-start(s32[144]{0:T(256)S(1)} %add_select_fusion.2), channel_id=1, source_target_pairs={{0,4},{1,5},{2,6},{3,7},{4,0},{5,1},{6,2},{7,3},{8,12},{9,13},{10,... | collective-permute-start | bytes 1736 | tf_op jit(solution)/shard_map/ppermute | solution.py:596
  84.7 19.3 %collective-permute-start.3 = (s32[288]{0:T(512)S(1)}, s32[288]{0:T(512)S(1)}, u32[]{:S(2)}, u32[]{:S(2)}) collective-permute-start(s32[288]{0:T(512)S(1)} %add_select_fusion.1), channel_id=1, source_target_pairs={{0,8},{1,9},{2,10},{3,11},{4,12},{5,13},{6,14},{7,15},{8,0},{9,1},... | collective-permute-start | bytes 3464 | tf_op jit(solution)/shard_map/ppermute | solution.py:596
  114.0 82.4 %collective-permute-start.4 = (bf16[1024,512]{1,0:T(8,128)(2,1)}, bf16[1024,512]{1,0:T(8,128)(2,1)}, u32[]{:S(2)}, u32[]{:S(2)}) collective-permute-start(bf16[1024,512]{1,0:T(8,128)(2,1)} %bitcast.24), channel_id=1, source_target_pairs={{0,4},{4,8},{8,12},{12,13},{13,9},{9,5},{5,1},{1,3},{3,7},{7,11},{... | collective-permute-start | bytes 3145736 | tf_op jit(solution)/shard_map/ppermute | solution.py:627
  116.8 79.7 %collective-permute-start.5 = (bf16[1024,512]{1,0:T(8,128)(2,1)}, bf16[1024,512]{1,0:T(8,128)(2,1)}, u32[]{:S(2)}, u32[]{:S(2)}) collective-permute-start(bf16[1024,512]{1,0:T(8,128)(2,1)} %bitcast.21), channel_id=1, source_target_pairs={{0,2},{4,0},{8,4},{12,8},{13,12},{9,13},{5,9},{1,5},{3,1},{7,3},{1... | collective-permute-start | bytes 3145736 | tf_op jit(solution)/shard_map/ppermute | solution.py:628
  116.8 132.1 %collective-permute-start.6 = (bf16[1024,512]{1,0:T(8,128)(2,1)}, bf16[1024,512]{1,0:T(8,128)(2,1)S(1)}, u32[]{:S(2)}, u32[]{:S(2)}) collective-permute-start(bf16[1024,512]{1,0:T(8,128)(2,1)} %bitcast.18), channel_id=1, source_target_pairs={{0,4},{4,8},{8,12},{12,13},{13,9},{9,5},{5,1},{1,3},{3,7},{7,11},{... | collective-permute-start | bytes 3145736 | tf_op jit(solution)/shard_map/ppermute | solution.py:627
  118.8 130.1 %collective-permute-start.7 = (bf16[1024,512]{1,0:T(8,128)(2,1)}, bf16[1024,512]{1,0:T(8,128)(2,1)}, u32[]{:S(2)}, u32[]{:S(2)}) collective-permute-start(bf16[1024,512]{1,0:T(8,128)(2,1)} %bitcast.15), channel_id=1, source_target_pairs={{0,2},{4,0},{8,4},{12,8},{13,12},{9,13},{5,9},{1,5},{3,1},{7,3},{1... | collective-permute-start | bytes 3145736 | tf_op jit(solution)/shard_map/ppermute | solution.py:628
  248.9 1.0 copy-start.2
  305.9 139.6 %all-to-all-start.1 = ((bf16[32,1,64,512]{3,2,1,0:T(8,128)(2,1)}), bf16[32,1,64,512]{3,2,1,0:T(8,128)(2,1)}, u32[]{:S(2)}, u32[]{:S(2)}) async-start(bf16[32,1,64,512]{3,2,1,0:T(8,128)(2,1)} %get-tuple-element.56), calls=%async_computation.1 | async-start | bytes 4194304 | tf_op jit(solution)/shard_map/all_to_all | solution.py:603
  445.5 53.1 %all-to-all-start.2 = ((bf16[32,1,64,512]{3,2,1,0:T(8,128)(2,1)}), bf16[32,1,64,512]{3,2,1,0:T(8,128)(2,1)}, u32[]{:S(2)}, u32[]{:S(2)}) async-start(bf16[32,1,64,512]{3,2,1,0:T(8,128)(2,1)} %rest.1), calls=%async_computation.2 | async-start | bytes 4194304 | tf_op jit(solution)/shard_map/all_to_all | solution.py:603

commit v6 on v4

--- a/solution.py
+++ b/solution.py
@@ -243,7 +243,7 @@
 
 def home_sum(blocks, part, slots, start, result=None):
     block_count = blocks.shape[0]
-    group = 4
+    group = 8
     chunk_shape = (block_count,) + part.shape[1:]
     operands = (slots, blocks, part) + (() if result is None else (result,))
     return pl.pallas_call(

time: 503 us -> 503 us (level)
  no operation moved by 1% of the time
where the time goes in v6:
time: 503 us; the launch traced here: 502 us
  Pallas kernels  340 us (68%)
  waiting for transfers between devices  127 us (25%)
  starting transfers between devices  30.4 us (6%)
    pallas_call x1, Pallas kernels, rest_attention(): pl.pallas_call(rest_kernel, grid_spec=pltpu.PrefetchScalarGridSpec(num_sc...  134 us
    pallas_call x2, Pallas kernels, partner_chunk(): pl.pallas_call(functools.partial(partner_kernel, last=last), grid_spec=pl...  108 us
    ppermute x4, waiting for transfers between devices, told_by_all(): lax.ppermute(told, 'seq', [(place, place ^ step) for place in range(shard...  81.5 us
    pallas_call x1, Pallas kernels, own_attention(): pl.pallas_call(own_kernel, grid=(patch_count,), in_specs=[pl.BlockSpec((c...  77.6 us
    all_to_all x3, waiting for transfers between devices, exchanged(): return lax.all_to_all(value, 'seq', split_axis=0, concat_axis=0, tiled=True)  46 us
    all_to_all x3, starting transfers between devices, exchanged(): return lax.all_to_all(value, 'seq', split_axis=0, concat_axis=0, tiled=True)  20.1 us
  transfers between devices with their start and end apart: 11, of which 6 were waited for; matrix products, arithmetic and copies ran while one was open for 1% of the time, Pallas kernels for 53%

profile of v6, /device:TPU:12, one launch (start us, length us, event | category | flops | bytes accessed | tf_op | source)
XLA Modules:
  0.0 502.3 jit_solution(1010736325312290217)
XLA Ops:
  0.0 6.6 %send.1 = (bf16[32,128,512]{2,1,0:T(8,128)(2,1)}, s32[32]{0:T(128)}, s32[36]{0:T(128)}) custom-call(s32[32]{0:T(128)} %order_ref.1, s32[4]{0:T(128)} %offsets_ref.1, s32[16]{0:T(128)} %constant.18.clone.places_ref, bf16[32,128,512]{2,1,0:T(8,128)(2,1)} %bitcast.11, f32[1,512]{1,0:T(1,128)} %bitcast.14), custom_call_target="tpu_custom_call" | custom-call | tf_op jit(solution)/shard_map/send/pallas_call | solution.py:107
  6.7 0.0 copy-start.1
  6.7 0.0 copy-start
  6.7 7.3 %all-to-all-start = ((bf16[32,128,512]{2,1,0:T(8,128)(2,1)}), bf16[32,128,512]{2,1,0:T(8,128)(2,1)}, u32[]{:S(2)}, u32[]{:S(2)}) async-start(bf16[32,128,512]{2,1,0:T(8,128)(2,1)} %get-tuple-element.34), calls=%async_computation | async-start | bytes 8388608 | tf_op jit(solution)/shard_map/all_to_all | solution.py:606
  14.0 0.0 copy-done.1
  14.0 1.5 collective-permute-start
  15.5 12.8 %collective-permute-done = s32[36]{0:T(128)S(1)} collective-permute-done((s32[36]{0:T(128)S(1)}, s32[36]{0:T(128)S(1)}, u32[]{:S(2)}, u32[]{:S(2)}) %collective-permute-start) | collective-permute-done | bytes 176 | tf_op jit(solution)/shard_map/ppermute | solution.py:599
  28.3 0.1 broadcast_select_fusion
  28.4 0.7 collective-permute-start.1
  29.1 2.9 collective-permute-done.1
  32.0 0.1 add_select_fusion.2
  32.1 1.4 collective-permute-start.2
  33.4 0.0 copy-done
  33.4 1.0 fusion
  34.5 0.2 copy.13
  34.7 0.2 copy.12
  34.9 49.7 %collective-permute-done.2 = s32[144]{0:T(256)S(1)} collective-permute-done((s32[144]{0:T(256)S(1)}, s32[144]{0:T(256)S(1)}, u32[]{:S(2)}, u32[]{:S(2)}) %collective-permute-start.2) | collective-permute-done | bytes 608 | tf_op jit(solution)/shard_map/ppermute | solution.py:599
  84.6 0.1 add_select_fusion.1
  84.7 2.1 collective-permute-start.3
  86.8 1.0 maximum_bitcast_fusion.wqv_ref.refs_9_
  87.8 16.1 %collective-permute-done.3 = s32[288]{0:T(512)S(1)} collective-permute-done((s32[288]{0:T(512)S(1)}, s32[288]{0:T(512)S(1)}, u32[]{:S(2)}, u32[]{:S(2)}) %collective-permute-start.3) | collective-permute-done | bytes 1184 | tf_op jit(solution)/shard_map/ppermute | solution.py:599
  104.0 0.7 add_select_fusion.known_ref
  104.6 3.6 all-to-all-done
  108.3 5.3 %sort.1 = (bf16[2,1,8,64,512]{4,3,2,1,0:T(8,128)(2,1)}, bf16[2,1,8,64,512]{4,3,2,1,0:T(8,128)(2,1)}, bf16[2,1,8,64,512]{4,3,2,1,0:T(8,128)(2,1)}, bf16[2,1,8,64,...) custom-call(s32[576]{0:T(1024)} %add_select_fusion.known_ref, s32[16]{0:T(128)} %constant.19.clone.ranges_ref, ...), custom_call_target="tpu_custom_call" | custom-call | tf_op jit(solution)/shard_map/sort/pallas_call | solution.py:189
  113.5 2.6 collective-permute-start.4
  116.1 0.0 collective-permute-start.5
  116.1 2.0 collective-permute-start.6
  118.1 0.0 collective-permute-start.7
  118.1 77.6 %own.1 = (bf16[512,2048]{1,0:T(8,128)(2,1)}, bf16[512,2048]{1,0:T(8,128)(2,1)}, bf16[4096,512]{1,0:T(8,128)(2,1)}, bf16[512,4096]{1,0:T(8,128)(2,1)}, f32[512,20...) custom-call(bf16[1024,512]{1,0:T(8,128)(2,1)} %bitcast.22, bf16[1024,512]{1,0:T(8,128)(2,1)} %bitcast.25, ...), custom_call_target="tpu_custom_call" | custom-call | flops 25999998976 | bytes 28000000 | tf_op jit(solution)/shard_map/own/pallas_call | solution.py:469
  195.8 0.0 collective-permute-done.4.refs_0_
  195.8 0.0 collective-permute-done.5.refs_3_
  195.8 52.4 %partner_next.1 = (bf16[2048,512]{1,0:T(8,128)(2,1)}, bf16[512,2048]{1,0:T(8,128)(2,1)}, f32[512,2048]{1,0:T(8,128)}, f32[8,2048]{1,0:T(8,128)}, f32[8,2048]{1,0:T(8,128)}) custom-call(s32[32]{0:T(128)} %get-tuple-element.35.picked_ref, s32[4]{0:T(128)} %get-tuple-element.43.source_ref, s32[4]{0:T(128)} %get-tuple-element.44.within_ref, ...), custom_call_target="tpu_custom_call" | custom-call | flops 15000000512 | bytes 28000000 | tf_op jit(solution)/shard_map/partner_next/pallas_call | solution.py:548
  248.2 0.0 collective-permute-done.6.refs_0_
  248.2 0.0 copy-start.2
  248.2 0.0 collective-permute-done.7.refs_3_
  248.2 1.0 copy-done.2
  249.2 56.0 %partner_last.1 = (bf16[32,1,64,512]{3,2,1,0:T(8,128)(2,1)}, bf16[2048,512]{1,0:T(8,128)(2,1)}, bf16[512,2048]{1,0:T(8,128)(2,1)}) custom-call(s32[32]{0:T(128)} %get-tuple-element.35.picked_ref, s32[4]{0:T(128)} %get-tuple-element.43.source_ref, s32[4]{0:T(128)} %get-tuple-element.44.within_ref, bf16[1024,512]{1,0:T(8,128)(2,1)} %copy-done.2, ...), custom_call_target="tpu_custom_call" | custom-call | flops 15000000512 | bytes 28000000 | tf_op jit(solution)/shard_map/partner_last/pallas_call | solution.py:548
  305.2 5.8 %all-to-all-start.1 = ((bf16[32,1,64,512]{3,2,1,0:T(8,128)(2,1)}), bf16[32,1,64,512]{3,2,1,0:T(8,128)(2,1)}, u32[]{:S(2)}, u32[]{:S(2)}) async-start(bf16[32,1,64,512]{3,2,1,0:T(8,128)(2,1)} %get-tuple-element.56), calls=%async_computation.1 | async-start | bytes 4194304 | tf_op jit(solution)/shard_map/all_to_all | solution.py:606
  311.1 133.8 %rest.1 = bf16[32,1,64,512]{3,2,1,0:T(8,128)(2,1)} custom-call(s32[32]{0:T(128)} %get-tuple-element.35.picked_ref, bf16[512,2048]{1,0:T(8,128)(2,1)} %get-tuple-element.40.query_ref, bf16[4096,512]{1,0:T(8,128)(2,1)} %get-tuple-element.41.refs_0_, bf16[512,4096]{1,0:T(8,128)(2,1)} %get-tuple-element.42.refs_1_, bf16[2048,512]{1,0:T(8,128)(2,1)} %get-tuple-element.49.refs_2_, ...), custom_call_target="tpu_custom_call" | custom-call | flops 38000001024 | bytes 28000000 | tf_op jit(solution)/shard_map/rest/pallas_call | solution.py:576
  444.9 0.0 all-to-all-done.1.part_ref
  444.9 6.9 %all-to-all-start.2 = ((bf16[32,1,64,512]{3,2,1,0:T(8,128)(2,1)}), bf16[32,1,64,512]{3,2,1,0:T(8,128)(2,1)}, u32[]{:S(2)}, u32[]{:S(2)}) async-start(bf16[32,1,64,512]{3,2,1,0:T(8,128)(2,1)} %rest.1), calls=%async_computation.2 | async-start | bytes 4194304 | tf_op jit(solution)/shard_map/all_to_all | solution.py:606
  451.8 4.0 home.2.refs_0_
  455.8 42.3 %all-to-all-done.2.part_ref = bf16[32,1,64,512]{3,2,1,0:T(8,128)(2,1)} async-done(((bf16[32,1,64,512]{3,2,1,0:T(8,128)(2,1)}), bf16[32,1,64,512]{3,2,1,0:T(8,128)(2,1)}, u32[]{:S(2)}, u32[]{:S(2)}) %all-to-all-start.2) | async-done | bytes 2097184 | tf_op jit(solution)/shard_map/all_to_all | solution.py:606
  498.1 4.0 home.3
Async XLA Ops:
  6.7 7.3 %copy-start.1 = (s32[36]{0:T(128)S(1)}, s32[36]{0:T(128)}, u32[]{:S(2)}) copy-start(s32[36]{0:T(128)} %get-tuple-element.33) | copy-start | bytes 436
  6.7 26.8 %copy-start = (bf16[512,1536]{1,0:T(8,128)(2,1)S(1)}, bf16[512,1536]{1,0:T(8,128)(2,1)}, u32[]{:S(2)}) copy-start(bf16[512,1536]{1,0:T(8,128)(2,1)} %param.12) | copy-start | bytes 4718596
  6.7 101.6 %all-to-all-start = ((bf16[32,128,512]{2,1,0:T(8,128)(2,1)}), bf16[32,128,512]{2,1,0:T(8,128)(2,1)}, u32[]{:S(2)}, u32[]{:S(2)}) async-start(bf16[32,128,512]{2,1,0:T(8,128)(2,1)} %get-tuple-element.34), calls=%async_computation | async-start | bytes 8388608 | tf_op jit(solution)/shard_map/all_to_all | solution.py:606
  14.0 14.3 %collective-permute-start = (s32[36]{0:T(128)S(1)}, s32[36]{0:T(128)S(1)}, u32[]{:S(2)}, u32[]{:S(2)}) collective-permute-start(s32[36]{0:T(128)S(1)} %copy-done.1), channel_id=1, source_target_pairs={{0,1},{1,0},{2,3},{3,2},{4,5},{5,4},{6,7},{7,6},{8,9},{9,8},{10,11... | collective-permute-start | bytes 440 | tf_op jit(solution)/shard_map/ppermute | solution.py:599
  28.4 3.6 collective-permute-start.1
  32.1 52.5 %collective-permute-start.2 = (s32[144]{0:T(256)S(1)}, s32[144]{0:T(256)S(1)}, u32[]{:S(2)}, u32[]{:S(2)}) collective-permute-start(s32[144]{0:T(256)S(1)} %add_select_fusion.2), channel_id=1, source_target_pairs={{0,4},{1,5},{2,6},{3,7},{4,0},{5,1},{6,2},{7,3},{8,12},{9,13},{10,... | collective-permute-start | bytes 1736 | tf_op jit(solution)/shard_map/ppermute | solution.py:599
  84.7 19.3 %collective-permute-start.3 = (s32[288]{0:T(512)S(1)}, s32[288]{0:T(512)S(1)}, u32[]{:S(2)}, u32[]{:S(2)}) collective-permute-start(s32[288]{0:T(512)S(1)} %add_select_fusion.1), channel_id=1, source_target_pairs={{0,8},{1,9},{2,10},{3,11},{4,12},{5,13},{6,14},{7,15},{8,0},{9,1},... | collective-permute-start | bytes 3464 | tf_op jit(solution)/shard_map/ppermute | solution.py:599
  113.5 82.2 %collective-permute-start.4 = (bf16[1024,512]{1,0:T(8,128)(2,1)}, bf16[1024,512]{1,0:T(8,128)(2,1)}, u32[]{:S(2)}, u32[]{:S(2)}) collective-permute-start(bf16[1024,512]{1,0:T(8,128)(2,1)} %bitcast.24), channel_id=1, source_target_pairs={{0,4},{4,8},{8,12},{12,13},{13,9},{9,5},{5,1},{1,3},{3,7},{7,11},{... | collective-permute-start | bytes 3145736 | tf_op jit(solution)/shard_map/ppermute | solution.py:630
  116.1 79.7 %collective-permute-start.5 = (bf16[1024,512]{1,0:T(8,128)(2,1)}, bf16[1024,512]{1,0:T(8,128)(2,1)}, u32[]{:S(2)}, u32[]{:S(2)}) collective-permute-start(bf16[1024,512]{1,0:T(8,128)(2,1)} %bitcast.21), channel_id=1, source_target_pairs={{0,2},{4,0},{8,4},{12,8},{13,12},{9,13},{5,9},{1,5},{3,1},{7,3},{1... | collective-permute-start | bytes 3145736 | tf_op jit(solution)/shard_map/ppermute | solution.py:631
  116.1 132.1 %collective-permute-start.6 = (bf16[1024,512]{1,0:T(8,128)(2,1)}, bf16[1024,512]{1,0:T(8,128)(2,1)S(1)}, u32[]{:S(2)}, u32[]{:S(2)}) collective-permute-start(bf16[1024,512]{1,0:T(8,128)(2,1)} %bitcast.18), channel_id=1, source_target_pairs={{0,4},{4,8},{8,12},{12,13},{13,9},{9,5},{5,1},{1,3},{3,7},{7,11},{... | collective-permute-start | bytes 3145736 | tf_op jit(solution)/shard_map/ppermute | solution.py:630
  118.1 130.1 %collective-permute-start.7 = (bf16[1024,512]{1,0:T(8,128)(2,1)}, bf16[1024,512]{1,0:T(8,128)(2,1)}, u32[]{:S(2)}, u32[]{:S(2)}) collective-permute-start(bf16[1024,512]{1,0:T(8,128)(2,1)} %bitcast.15), channel_id=1, source_target_pairs={{0,2},{4,0},{8,4},{12,8},{13,12},{9,13},{5,9},{1,5},{3,1},{7,3},{1... | collective-permute-start | bytes 3145736 | tf_op jit(solution)/shard_map/ppermute | solution.py:631
  248.2 1.0 copy-start.2
  305.2 139.7 %all-to-all-start.1 = ((bf16[32,1,64,512]{3,2,1,0:T(8,128)(2,1)}), bf16[32,1,64,512]{3,2,1,0:T(8,128)(2,1)}, u32[]{:S(2)}, u32[]{:S(2)}) async-start(bf16[32,1,64,512]{3,2,1,0:T(8,128)(2,1)} %get-tuple-element.56), calls=%async_computation.1 | async-start | bytes 4194304 | tf_op jit(solution)/shard_map/all_to_all | solution.py:606
  444.9 53.3 %all-to-all-start.2 = ((bf16[32,1,64,512]{3,2,1,0:T(8,128)(2,1)}), bf16[32,1,64,512]{3,2,1,0:T(8,128)(2,1)}, u32[]{:S(2)}, u32[]{:S(2)}) async-start(bf16[32,1,64,512]{3,2,1,0:T(8,128)(2,1)} %rest.1), calls=%async_computation.2 | async-start | bytes 4194304 | tf_op jit(solution)/shard_map/all_to_all | solution.py:606
